TPU v7x, 128 devices: a whole 4x4x4 slice. The times are simulated.
128 devices in a mesh: seq: 32 (over z, y, core), ch: 4 (over x).
Axes of the slice: x: 4, y: 4, z: 4, core: 2. Of those that a mesh axis runs over, the one named last changes fastest.
Arguments:
- hidden: bfloat16 [16384, 1024], P('seq'), may hold values from -6 to 6
- proj_x: bfloat16 [1024, 2048], P(None, 'ch'), may hold values from -0.1875 to 0.1875
- proj_z: bfloat16 [1024, 2048], P(None, 'ch'), may hold values from -0.1875 to 0.1875
- proj_b: bfloat16 [1024, 16], replicated, may hold values from -0.005859375 to 0.005859375
- proj_c: bfloat16 [1024, 16], replicated, may hold values from -0.046875 to 0.046875
- proj_dt: bfloat16 [1024, 32], P(None, 'ch'), may hold values from -0.1875 to 0.1875
- dt_bias: float32 [32], P('ch'), may hold values from -2 to 0.5
- decay_rate: float32 [32], P('ch'), may hold values from 0 to 1, as said below
- skip_gain: float32 [32], P('ch'), may hold values from 0.5 to 1.5
- proj_out: bfloat16 [2048, 1024], P('ch'), may hold values from -0.125 to 0.125
- cotangent: bfloat16 [16384, 1024], P('seq', 'ch'), may hold values from -6 to 6
Outputs:
- block_out: bfloat16 [16384, 1024], P('seq', 'ch')
- grad_hidden: float32 [16384, 1024], P('seq', 'ch')
- grad_proj_x: float32 [1024, 2048], P('seq', 'ch')
- grad_proj_z: float32 [1024, 2048], P('seq', 'ch')
- grad_proj_out: float32 [2048, 1024], P('ch', 'seq')
Inputs may be any that keep to these rules, and one draw needn't show every extreme that they name: `decay_rate`: positive rates.
All inputs are finite; a program needn't handle non-finite values.
Results may differ from a plain program's by a relative error of at most 0.0055.
Values may be sent and summed in bfloat16 or wider, within the bound.
A program may use at most 256 MiB of HBM per device.

v0:
```python
import functools

import jax
import jax.numpy as jnp
from jax import lax
from jax.experimental import pallas as pl
from jax.experimental.pallas import tpu as pltpu
from jax.sharding import PartitionSpec as P

L = 512
D = 1024
W = 512
HEADS = 8
HEAD = 64
NS = 16
Q = 256
CHUNKS = L // Q
NSEQ = 32
F32 = jnp.float32
BF16 = jnp.bfloat16

LAST = (((1,), (1,)), ((), ()))
FIRST = (((0,), (0,)), ((), ()))


def mm(a, b):
    return jnp.dot(a, b, preferred_element_type=F32)


def mm_t(a, b):
    return lax.dot_general(a, b, LAST, preferred_element_type=F32)


def t_mm(a, b):
    return lax.dot_general(a, b, FIRST, preferred_element_type=F32)


def split2(v):
    high = v.astype(BF16)
    return high, (v - high.astype(F32)).astype(BF16)


def split3(v):
    high = v.astype(BF16)
    rest = v - high.astype(F32)
    mid = rest.astype(BF16)
    return high, mid, (rest - mid.astype(F32)).astype(BF16)


def iota(shape, dim):
    return lax.broadcasted_iota(jnp.int32, shape, dim)


def anti_identity():
    return jnp.where(iota((Q, Q), 0) + iota((Q, Q), 1) == Q - 1, 1.0, 0.0).astype(BF16)


def spread_matrix():
    return jnp.where(iota((HEADS, W), 1) // HEAD == iota((HEADS, W), 0), 1.0, 0.0).astype(BF16)


def spread(v, e):
    high, low = split2(v)
    return mm(high, e) + mm(low, e)


def gather_heads(v, e):
    high, low = split2(v)
    return mm_t(high, e) + mm_t(low, e)


def order(strand, transposed=False):
    rows, columns = iota((Q, Q), 0), iota((Q, Q), 1)
    later = strand == 0
    if transposed:
        later = not later
    return rows >= columns if later else rows <= columns


def running(v, mask):
    ones = jnp.where(mask, 1.0, 0.0).astype(BF16)
    return sum(mm(ones, part) for part in split3(v))


def softplus(v):
    return jnp.maximum(v, 0.0) + jnp.log1p(jnp.exp(-jnp.abs(v)))


def sigmoid(v):
    return 1.0 / (1.0 + jnp.exp(-v))


def flip_columns(src, dst, anti):
    n = src.shape[1] // Q
    for k in range(n):
        dst[:, k * Q : (k + 1) * Q] = mm(src[:, (n - 1 - k) * Q : (n - k) * Q], anti).astype(BF16)


def flip_rows(src, dst, anti):
    n = src.shape[0] // Q
    for k in range(n):
        dst[k * Q : (k + 1) * Q, :] = mm(anti, src[(n - 1 - k) * Q : (n - k) * Q, :]).astype(BF16)


def project_kernel(
    hidden, proj_x, proj_z, proj_b, proj_c, proj_dt, bias, rate, proj_out, cot,
    xs, zs, bs, cs, dts, dos, hidden_flip, cot_flip, px_flip, pz_flip, pb_flip, pc_flip, pd_flip, po_flip,
    state_out,
    decay_out,
):
    anti = anti_identity()
    e = spread_matrix()
    flip_rows(proj_x, px_flip, anti)
    flip_rows(proj_z, pz_flip, anti)
    flip_rows(proj_b, pb_flip, anti)
    flip_rows(proj_c, pc_flip, anti)
    flip_rows(proj_dt, pd_flip, anti)
    flip_columns(proj_out, po_flip, anti)
    flip_columns(hidden, hidden_flip, anti)
    flip_columns(cot, cot_flip, anti)
    weights = (
        (proj_x, proj_z, proj_b, proj_c, proj_dt, proj_out),
        (px_flip, pz_flip, pb_flip, pc_flip, pd_flip, po_flip),
    )
    for strand in range(2):
        w_x, w_z, w_b, w_c, w_dt, w_out = weights[strand]

        def rows_step(k, carry):
            rows = pl.ds(pl.multiple_of(k * Q, Q), Q)
            u = hidden[rows, :]
            xs[strand, rows, :] = mm(u, w_x[...])
            zs[strand, rows, :] = mm(u, w_z[...])
            bs[strand, rows, :] = mm(u, w_b[...])
            cs[strand, rows, :] = mm(u, w_c[...])
            dts[strand, rows, :] = mm(u, w_dt[...])
            dos[strand, rows, :] = mm_t(cot[rows, :], w_out[...]).astype(BF16)
            return carry

        lax.fori_loop(0, CHUNKS, rows_step, 0)

        def state_step(i, carry):
            k = i if strand == 0 else CHUNKS - 1 - i
            rows = pl.ds(pl.multiple_of(k * Q, Q), Q)
            state, grad, before = carry
            dt = softplus(dts[strand, rows, :] + bias[...])
            a = -rate[...] * dt
            cum = running(a, order(strand))
            total = jnp.sum(a, axis=0, keepdims=True)
            z = zs[strand, rows, :]
            dy = dos[strand, rows, :].astype(F32) * (z * sigmoid(z))
            weighted = (xs[strand, rows, :] * spread(jnp.exp(total - cum) * dt, e)).astype(BF16)
            local = t_mm(bs[strand, rows, :].astype(BF16), weighted)
            dyw = (dy * spread(jnp.exp(cum), e)).astype(BF16)
            local_grad = t_mm(cs[strand, rows, :].astype(BF16), dyw)
            here = jnp.exp(spread(total, e))
            return (here * state + local, grad + before * local_grad, before * here)

        zero = jnp.zeros((NS, W), F32)
        state, grad, decay = lax.fori_loop(
            0, CHUNKS, state_step, (zero, zero, jnp.ones((1, W), F32))
        )
        state_out[2 * strand] = state
        state_out[2 * strand + 1] = grad
        decay_out[strand] = jnp.broadcast_to(decay, (8, W))


def scan_kernel(
    hidden, proj_x, proj_z, proj_b, proj_c, proj_dt, bias, rate, skip, proj_out, cot,
    xs, zs, bs, cs, dts, dos, hidden_flip, cot_flip, px_flip, pz_flip, pb_flip, pc_flip, pd_flip, po_flip,
    states, decays,
    mix, grad_in, grad_w, grad_out,
    os, dxs, dzs, dbs, dcs, ddts, yi, gi, dyb, xdt, zacc, chunk_state, chunk_grad, chunk_decay,
):
    e = spread_matrix()
    me = lax.axis_index("seq")
    skip_wide = spread(skip[...], e)
    weights = (
        (proj_x, proj_z, proj_b, proj_c, proj_dt, proj_out),
        (px_flip, pz_flip, pb_flip, pc_flip, pd_flip, po_flip),
    )
    zero = jnp.zeros((NS, W), F32)
    for strand in range(2):
        w_x, w_z, w_b, w_c, w_dt, w_out = weights[strand]
        rising = strand == 0

        def up(j, carry, kind):
            new = carry * decays[j, strand, 0:1, :] + states[j, 2 * strand + kind]
            return jnp.where(j < me, new, carry)

        def down(i, carry, kind):
            j = NSEQ - 1 - i
            new = carry * decays[j, strand, 0:1, :] + states[j, 2 * strand + kind]
            return jnp.where(j > me, new, carry)

        state_in = lax.fori_loop(0, NSEQ, functools.partial(up if rising else down, kind=0), zero)
        grad_end = lax.fori_loop(0, NSEQ, functools.partial(down if rising else up, kind=1), zero)

        def inner_step(k, carry):
            rows = pl.ds(pl.multiple_of(k * Q, Q), Q)
            mask = order(strand)
            dt = softplus(dts[strand, rows, :] + bias[...])
            a = -rate[...] * dt
            cum = running(a, mask)
            cum_t = cum.T
            total = jnp.sum(a, axis=0, keepdims=True)
            z = zs[strand, rows, :]
            dy = dos[strand, rows, :].astype(F32) * (z * sigmoid(z))
            x = xs[strand, rows, :]
            xd = x * spread(dt, e)
            dyb[...] = dy.astype(BF16)
            xdt[...] = xd.astype(BF16)
            b = bs[strand, rows, :].astype(BF16)
            c = cs[strand, rows, :].astype(BF16)
            scores = mm_t(c, b)
            lane = iota((Q, 128), 1)
            for pair in range(HEADS // 2):
                columns = slice(pair * 128, (pair + 1) * 128)
                y_pair = None
                for half in range(2):
                    h = 2 * pair + half
                    own = (lane >= 64) if half else (lane < 64)
                    x_own = jnp.where(own, xdt[:, columns], jnp.zeros((), BF16))
                    dy_own = jnp.where(own, dyb[:, columns], jnp.zeros((), BF16))
                    decay = jnp.exp(
                        jnp.where(mask, cum[:, h : h + 1] - cum_t[h : h + 1, :], -1e30)
                    )
                    cross = mm_t(dy_own, xdt[:, columns])
                    mixing = (decay * scores).astype(BF16)
                    if h == 0:
                        zacc[...] = decay * cross
                    else:
                        zacc[...] += decay * cross
                    y_new, g_new = mm(mixing, x_own), t_mm(mixing, dy_own)
                    y_pair, g_pair = (
                        (y_new, g_new) if y_pair is None else (y_pair + y_new, g_pair + g_new)
                    )
                yi[rows, columns] = y_pair
                gi[rows, columns] = g_pair
            both = zacc[...].astype(BF16)
            dcs[rows, :] = mm(both, b)
            dbs[rows, :] = t_mm(both, c)
            e_cum = spread(jnp.exp(cum), e)
            e_rest = spread(jnp.exp(total - cum), e)
            here = jnp.exp(spread(total, e))
            chunk_state[k] = t_mm(b, (xd * e_rest).astype(BF16))
            chunk_grad[k] = t_mm(c, (dy * e_cum).astype(BF16))
            chunk_decay[k] = jnp.broadcast_to(here, (8, W))
            return carry

        lax.fori_loop(0, CHUNKS, inner_step, 0)

        times = list(range(CHUNKS)) if rising else list(range(CHUNKS))[::-1]
        entering, leaving, leaving_grad = {}, {}, {}
        state = state_in
        for k in times:
            entering[k] = state
            state = chunk_decay[k, 0:1, :] * state + chunk_state[k]
            leaving[k] = state
        grad = grad_end
        for k in times[::-1]:
            leaving_grad[k] = grad
            grad = chunk_decay[k, 0:1, :] * grad + chunk_grad[k]
        for k in range(CHUNKS):
            chunk_state[k] = entering[k]
            chunk_grad[k] = leaving_grad[k]
            chunk_decay[k] = jnp.broadcast_to(
                jnp.sum(leaving[k] * leaving_grad[k], axis=0, keepdims=True), (8, W)
            )

        def outer_step(k, carry):
            rows = pl.ds(pl.multiple_of(k * Q, Q), Q)
            mask = order(strand)
            raw = dts[strand, rows, :] + bias[...]
            dt = softplus(raw)
            a = -rate[...] * dt
            cum = running(a, mask)
            total = jnp.sum(a, axis=0, keepdims=True)
            e_cum = spread(jnp.exp(cum), e)
            e_rest = spread(jnp.exp(total - cum), e)
            dt_wide = spread(dt, e)
            b = bs[strand, rows, :].astype(BF16)
            c = cs[strand, rows, :].astype(BF16)
            state = chunk_state[k].astype(BF16)
            grad = chunk_grad[k].astype(BF16)
            x = xs[strand, rows, :]
            z = zs[strand, rows, :]
            d_o = dos[strand, rows, :].astype(F32)
            sig = sigmoid(z)
            silu = z * sig
            dy = d_o * silu
            y_part = yi[rows, :] + e_cum * mm(c, state)
            gb = gi[rows, :] + e_rest * mm(b, grad)
            y = y_part + skip_wide * x
            os[strand, rows, :] = (y * silu).astype(BF16)
            dzs[strand, rows, :] = (d_o * y * (sig + silu * (1.0 - sig))).astype(BF16)
            dxs[strand, rows, :] = (dt_wide * gb + skip_wide * dy).astype(BF16)
            d_c = dcs[rows, :] + mm_t((dy * e_cum).astype(BF16), state)
            d_b = dbs[rows, :] + mm_t((x * dt_wide * e_rest).astype(BF16), grad)
            direct = gather_heads(x * gb, e)
            d_cum = gather_heads(dy * y_part, e) - dt * direct
            d_a = running(d_cum, order(strand, True)) + gather_heads(
                chunk_decay[k], e
            )[0:1, :]
            d_raw = (direct - rate[...] * d_a) * sigmoid(raw)
            extra = (
                mm_t(d_b.astype(BF16), w_b[...])
                + mm_t(d_c.astype(BF16), w_c[...])
                + mm_t(d_raw.astype(BF16), w_dt[...])
            )
            if strand == 0:
                grad_in[rows, :] = extra
            else:
                grad_in[rows, :] += extra
            grad_in[rows, :] += mm_t(dxs[strand, rows, :], w_x[...]) + mm_t(
                dzs[strand, rows, :], w_z[...]
            )
            part = mm(os[strand, rows, :], w_out[...])
            if strand == 0:
                mix[rows, :] = part
            else:
                mix[rows, :] += part
            return carry

        lax.fori_loop(0, CHUNKS, outer_step, 0)

    def weight_step(k, carry):
        cols = pl.ds(pl.multiple_of(k * Q, Q), Q)
        grad_w[cols, 0:W] = t_mm(hidden[:, cols], dxs[0]) + t_mm(hidden_flip[:, cols], dxs[1])
        grad_w[cols, W:] = t_mm(hidden[:, cols], dzs[0]) + t_mm(hidden_flip[:, cols], dzs[1])
        grad_out[cols, :] = t_mm(cot[:, cols], os[0]) + t_mm(cot_flip[:, cols], os[1])
        return carry

    lax.fori_loop(0, D // Q, weight_step, 0)


def shape(*dims, dtype=F32):
    return jax.ShapeDtypeStruct(dims, dtype)


VMEM = pl.BlockSpec(memory_space=pltpu.VMEM)


def body(
    hidden, proj_x, proj_z, proj_b, proj_c, proj_dt, dt_bias, decay_rate, skip_gain, proj_out, cotangent
):
    cot = lax.all_gather(cotangent, "ch", axis=1, tiled=True)
    bias, rate, skip = (v[None, :] for v in (dt_bias, decay_rate, skip_gain))
    saved_shapes = (
        shape(2, L, W),
        shape(2, L, W),
        shape(2, L, NS),
        shape(2, L, NS),
        shape(2, L, HEADS),
        shape(2, L, W, dtype=BF16),
        shape(L, D, dtype=BF16),
        shape(L, D, dtype=BF16),
        shape(D, W, dtype=BF16),
        shape(D, W, dtype=BF16),
        shape(D, NS, dtype=BF16),
        shape(D, NS, dtype=BF16),
        shape(D, HEADS, dtype=BF16),
        shape(W, D, dtype=BF16),
    )
    *saved, state, decay = pl.pallas_call(
        project_kernel,
        out_shape=saved_shapes + (shape(4, NS, W), shape(2, 8, W)),
        in_specs=[VMEM] * 10,
        out_specs=[VMEM] * 16,
        compiler_params=pltpu.CompilerParams(vmem_limit_bytes=56 * 2**20),
        name="project",
    )(hidden, proj_x, proj_z, proj_b, proj_c, proj_dt, bias, rate, proj_out, cot)
    states = lax.all_gather(state, "seq")
    decays = lax.all_gather(decay, "seq")
    mix, grad_in, grad_w, grad_out = pl.pallas_call(
        scan_kernel,
        out_shape=(shape(L, D), shape(L, D), shape(D, 2 * W), shape(D, W)),
        in_specs=[VMEM] * 27,
        out_specs=[VMEM] * 4,
        scratch_shapes=[
            pltpu.VMEM((2, L, W), BF16),
            pltpu.VMEM((2, L, W), BF16),
            pltpu.VMEM((2, L, W), BF16),
            pltpu.VMEM((L, NS), F32),
            pltpu.VMEM((L, NS), F32),
            pltpu.VMEM((L, HEADS), F32),
            pltpu.VMEM((L, W), F32),
            pltpu.VMEM((L, W), F32),
            pltpu.VMEM((Q, W), BF16),
            pltpu.VMEM((Q, W), BF16),
            pltpu.VMEM((Q, Q), F32),
            pltpu.VMEM((CHUNKS, NS, W), F32),
            pltpu.VMEM((CHUNKS, NS, W), F32),
            pltpu.VMEM((CHUNKS, 8, W), F32),
        ],
        compiler_params=pltpu.CompilerParams(vmem_limit_bytes=60 * 2**20),
        name="scan",
    )(
        hidden, proj_x, proj_z, proj_b, proj_c, proj_dt, bias, rate, skip, proj_out, cot,
        *saved, states, decays,
    )
    width = cotangent.shape[1]
    residual = lax.dynamic_slice_in_dim(hidden, lax.axis_index("ch") * width, width, 1)
    mixed = lax.psum_scatter(mix, "ch", scatter_dimension=1, tiled=True)
    block_out = (residual.astype(F32) + mixed).astype(BF16)
    grad_hidden = cotangent.astype(F32) + lax.psum_scatter(
        grad_in, "ch", scatter_dimension=1, tiled=True
    )
    both = lax.psum_scatter(grad_w, "seq", scatter_dimension=0, tiled=True)
    grad_proj_out = lax.psum_scatter(grad_out, "seq", scatter_dimension=0, tiled=True).T
    return (block_out, grad_hidden, both[:, :W], both[:, W:], grad_proj_out)


def solution(mesh):
    return jax.shard_map(
        body,
        mesh=mesh,
        in_specs=(
            P("seq", None),
            P(None, "ch"),
            P(None, "ch"),
            P(),
            P(),
            P(None, "ch"),
            P("ch"),
            P("ch"),
            P("ch"),
            P("ch", None),
            P("seq", "ch"),
        ),
        out_specs=(P("seq", "ch"), P("seq", "ch"), P("seq", "ch"), P("seq", "ch"), P("ch", "seq")),
        check_vma=False,
    )
```

profile of v0, /device:TPU:1, one launch (start us, length us, event | category | flops | bytes accessed | tf_op | source)
XLA Modules:
  0.0 421.9 jit_solution(15266604407966212282)
XLA Ops:
  7.2 0.0 all-gather.6.cloned.1.call-start
  7.2 0.7 all-gather.6.cloned.1.call-update
  7.9 0.0 all-gather.10.cloned.1.call-start
  7.9 1.6 copy.25.proj_b
  9.5 1.6 copy.26.proj_c
  11.1 1.6 copy.27.proj_dt
  12.7 25.2 %all-gather.6.cloned.1.call-done.cot = bf16[512,1024]{1,0:T(8,128)(2,1)} async-done(((bf16[512,256]{1,0:T(8,128)(2,1)}), bf16[512,1024]{1,0:T(8,128)(2,1)}) %all-gather.6.cloned.1.call-update) | async-done | bytes 1048592 | tf_op jit(solution)/shard_map/all_gather | solution.py:346
  37.9 18.0 %project.1 = (f32[2,512,512]{2,1,0:T(8,128)}, f32[2,512,512]{2,1,0:T(8,128)}, f32[2,512,16]{2,1,0:T(8,128)}, f32[2,512,16]{2,1,0:T(8,128)}, f32[2,512,8]{2,1,0:T...) custom-call(bf16[512,1024]{1,0:T(8,128)(2,1)} %hidden.3, ...), custom_call_target="tpu_custom_call" | custom-call | tf_op jit(solution)/shard_map/project/pallas_call | solution.py:364
  55.9 0.0 all-gather.10.cloned.1.call-update
  55.9 0.0 all-gather.8.cloned.1.call-start
  56.0 0.7 all-gather.8.cloned.1.call-update
  56.7 0.2 reduce-scatter.5.cloned.1.call-start
  56.9 44.4 %all-gather.10.cloned.1.call-done = f32[64,8,512]{2,1,0:T(8,128)} async-done(((f32[2,8,512]{2,1,0:T(8,128)}), f32[64,8,512]{2,1,0:T(8,128)}) %all-gather.10.cloned.1.call-update) | async-done | bytes 1048592 | tf_op jit(solution)/shard_map/all_gather | solution.py:373
  101.3 47.9 %all-gather.8.cloned.1.call-done = f32[128,16,512]{2,1,0:T(8,128)} async-done(((f32[4,16,512]{2,1,0:T(8,128)}), f32[128,16,512]{2,1,0:T(8,128)}) %all-gather.8.cloned.1.call-update) | async-done | bytes 4194320 | tf_op jit(solution)/shard_map/all_gather | solution.py:372
  149.2 38.8 %scan.1 = (f32[512,1024]{1,0:T(8,128)}, f32[512,1024]{1,0:T(8,128)}, f32[1024,1024]{1,0:T(8,128)}, f32[1024,512]{1,0:T(8,128)}) custom-call(bf16[512,1024]{1,0:T(8,128)(2,1)} %hidden.3, bf16[1024,512]{1,0:T(8,128)(2,1)} %proj_x.3, bf16[1024,512]{1,0:T(8,128)(2,1)} %proj_z.3, bf16[1024,16]{1,0:T(8,128)(2,1)} %copy.25.proj_b, bf16[1024,16]{1,0:T(8,128)(2,1)} %copy.26.proj_c, ...), custom_call_target="tpu_custom_call" | custom-call | tf_op jit(solution)/shard_map/scan/pallas_call | solution.py:374
  188.0 0.0 reduce-scatter.5.cloned.1.call-update
  188.0 0.0 reduce-scatter.7.cloned.1.call-start
  188.1 0.5 reduce-scatter.7.cloned.1.call-update
  188.6 0.0 reduce-scatter.9.cloned.1.call-start
  188.7 0.5 reduce-scatter.9.cloned.1.call-update
  189.2 0.0 copy-start
  189.2 0.0 reduce-scatter.11.cloned.1.call-start
  189.2 0.7 reduce-scatter.11.cloned.1.call-update
  190.0 26.8 %reduce-scatter.5.cloned.1.call-done = f32[512,256]{1,0:T(8,128)} async-done(((f32[512,1024]{1,0:T(8,128)}), f32[512,256]{1,0:T(8,128)}) %reduce-scatter.5.cloned.1.call-update) | async-done | bytes 524304 | tf_op jit(solution)/shard_map/reduce_scatter | solution.py:403
  216.7 1.9 add_convert_fusion
  218.6 29.9 %reduce-scatter.7.cloned.1.call-done = f32[512,256]{1,0:T(8,128)} async-done(((f32[512,1024]{1,0:T(8,128)}), f32[512,256]{1,0:T(8,128)}) %reduce-scatter.7.cloned.1.call-update) | async-done | bytes 524304 | tf_op jit(solution)/shard_map/reduce_scatter | solution.py:405
  248.5 0.0 copy-done
  248.5 1.9 convert_add_fusion
  250.4 81.9 %reduce-scatter.9.cloned.1.call-done = f32[32,1024]{1,0:T(8,128)} async-done(((f32[1024,1024]{1,0:T(8,128)}), f32[32,1024]{1,0:T(8,128)}) %reduce-scatter.9.cloned.1.call-update) | async-done | bytes 131088 | tf_op jit(solution)/shard_map/reduce_scatter | solution.py:408
  332.2 1.5 fusion
  333.8 81.3 %reduce-scatter.11.cloned.1.call-done = f32[32,512]{1,0:T(8,128)} async-done(((f32[1024,512]{1,0:T(8,128)}), f32[32,512]{1,0:T(8,128)}) %reduce-scatter.11.cloned.1.call-update) | async-done | bytes 65552 | tf_op jit(solution)/shard_map/reduce_scatter | solution.py:409
Async XLA Ops:
  7.2 30.7 %all-gather.6.cloned.1.call-start = ((), (), s32[]{:S(2)}) async-start(), calls=%async_computation.4 | async-start | bytes 1310720 | tf_op jit(solution)/shard_map/all_gather | solution.py:346
  7.9 93.4 %all-gather.10.cloned.1.call-start = ((), (), s32[]{:S(2)}) async-start(), calls=%async_computation.10 | async-start | bytes 1081344 | tf_op jit(solution)/shard_map/all_gather | solution.py:373
  55.9 93.3 %all-gather.8.cloned.1.call-start = ((), (), s32[]{:S(2)}) async-start(), calls=%async_computation.9 | async-start | bytes 4325376 | tf_op jit(solution)/shard_map/all_gather | solution.py:372
  56.7 160.1 %reduce-scatter.5.cloned.1.call-start = ((), (), s32[]{:S(2)}) async-start(), calls=%async_computation.5 | async-start | bytes 2621440 | tf_op jit(solution)/shard_map/reduce_scatter | solution.py:403
  188.0 60.5 %reduce-scatter.7.cloned.1.call-start = ((), (), s32[]{:S(2)}) async-start(), calls=%async_computation.6 | async-start | bytes 2621440 | tf_op jit(solution)/shard_map/reduce_scatter | solution.py:405
  188.6 143.6 %reduce-scatter.9.cloned.1.call-start = ((), (), s32[]{:S(2)}) async-start(), calls=%async_computation.7 | async-start | bytes 4325376 | tf_op jit(solution)/shard_map/reduce_scatter | solution.py:408
  189.2 59.3 %copy-start = (bf16[512,256]{1,0:T(8,128)(2,1)S(1)}, bf16[512,256]{1,0:T(8,128)(2,1)}, u32[]{:S(2)}) copy-start(bf16[512,256]{1,0:T(8,128)(2,1)} %param.21) | copy-start | bytes 786436
  189.2 225.9 %reduce-scatter.11.cloned.1.call-start = ((), (), s32[]{:S(2)}) async-start(), calls=%async_computation.8 | async-start | bytes 2162688 | tf_op jit(solution)/shard_map/reduce_scatter | solution.py:409
Sparse Core Ops, SparseCore 0:
  9.7 28.1 all-gather.5
  56.0 45.2 all-gather.9
  103.6 45.5 all-gather.7
  188.1 28.5 reduce-scatter.4
  219.1 29.3 reduce-scatter.6
  252.0 80.1 reduce-scatter.8
  336.8 78.2 reduce-scatter.10
where the time goes:
time: 423 us; the launch traced here: 422 us
  waiting for transfers between devices  340 us (80%)
  Pallas kernels  56.8 us (13%)
  between operations  14.1 us (3%)
  local copies, waits for them, and re-layouts  6.27 us (1%)
    reduce_scatter x1, waiting for transfers between devices, body(): both = lax.psum_scatter(grad_w, 'seq', scatter_dimension=0, tiled=True)  81.9 us
    reduce_scatter x1, waiting for transfers between devices, body(): lax.psum_scatter(grad_out, 'seq', scatter_dimension=0, tiled=True)  81.3 us
    all_gather x1, waiting for transfers between devices, body(): states = lax.all_gather(state, 'seq')  47.9 us
    all_gather x1, waiting for transfers between devices, body(): decays = lax.all_gather(decay, 'seq')  44.4 us
    pallas_call x1, Pallas kernels, body(): pl.pallas_call(scan_kernel, out_shape=(shape(L, D), shape(L, D), shape(D,...  38.8 us
    reduce_scatter x1, waiting for transfers between devices, body(): lax.psum_scatter(grad_in, 'ch', scatter_dimension=1, tiled=True)  29.9 us
    reduce_scatter x1, waiting for transfers between devices, body(): mixed = lax.psum_scatter(mix, 'ch', scatter_dimension=1, tiled=True)  26.8 us
    all_gather x1, waiting for transfers between devices, body(): cot = lax.all_gather(cotangent, 'ch', axis=1, tiled=True)  25.2 us
  transfers between devices with their start and end apart: 7, of which 7 were waited for; matrix products, arithmetic and copies ran while one was open for 2% of the time, Pallas kernels for 0%

commit v1 on v0

v1 whole, which is shorter than its diff:
```python
import jax
import jax.numpy as jnp
from jax import lax
from jax.experimental import pallas as pl
from jax.experimental.pallas import tpu as pltpu
from jax.sharding import PartitionSpec as P

L = 512
D = 1024
W = 512
HEADS = 8
HEAD = 64
NS = 16
Q = 256
CHUNKS = L // Q
BLOCKS = D // Q
PEERS = 16
ROWS = 32
F32 = jnp.float32
BF16 = jnp.bfloat16
MESH = pl.DeviceIdType.MESH

LAST = (((1,), (1,)), ((), ()))
FIRST = (((0,), (0,)), ((), ()))

SMALL = ((0, 16, 32), (48, 64, 80))

S_COT, S_CORE, S_Y, S_Z = 0, 3, 4, 7
S_MIX, S_IN, S_GCORE, S_GPEER = 10, 16, 22, 25
S_ALL = S_GPEER + 3 * PEERS


def mm(a, b):
    return jnp.dot(a, b, preferred_element_type=F32)


def mm_t(a, b):
    return lax.dot_general(a, b, LAST, preferred_element_type=F32)


def t_mm(a, b):
    return lax.dot_general(a, b, FIRST, preferred_element_type=F32)


def split2(v):
    high = v.astype(BF16)
    return high, (v - high.astype(F32)).astype(BF16)


def split3(v):
    high = v.astype(BF16)
    rest = v - high.astype(F32)
    mid = rest.astype(BF16)
    return high, mid, (rest - mid.astype(F32)).astype(BF16)


def iota(shape, dim):
    return lax.broadcasted_iota(jnp.int32, shape, dim)


def anti_identity():
    return jnp.where(iota((Q, Q), 0) + iota((Q, Q), 1) == Q - 1, 1.0, 0.0).astype(BF16)


def spread_matrix():
    return jnp.where(iota((HEADS, W), 1) // HEAD == iota((HEADS, W), 0), 1.0, 0.0).astype(BF16)


def spread(v, e):
    high, low = split2(v)
    return mm(high, e) + mm(low, e)


def gather_heads(v, e):
    high, low = split2(v)
    return mm_t(high, e) + mm_t(low, e)


def order(sign):
    return (iota((Q, Q), 0) - iota((Q, Q), 1)) * sign >= 0


def running(v, mask):
    ones = jnp.where(mask, 1.0, 0.0).astype(BF16)
    return sum(mm(ones, part) for part in split3(v))


def softplus(v):
    return jnp.maximum(v, 0.0) + jnp.log1p(jnp.exp(-jnp.abs(v)))


def sigmoid(v):
    return 1.0 / (1.0 + jnp.exp(-v))


def rows_of(k):
    return pl.ds(pl.multiple_of(k * Q, Q), Q)


def block_kernel(
    hidden, proj_x, proj_z, proj_b, proj_c, proj_dt, bias, rate, skip, proj_out, cotangent,
    block_out, grad_hidden, grad_x, grad_z, grad_out,
    px_flip, pz_flip, po_flip, small, hidden_flip, cot, cot_flip,
    xs, zs, bs, cs, dts, dos, cums, dts_soft, e_cums, e_rests, dt_wides, dyb, xdt, zacc,
    yi, gi, dcs, dbs, ext, os, dxs, dzs,
    chunk_state, chunk_grad, chunk_decay, chunk_dot,
    msg, msg_core, ybuf, zbuf, pair_msg, y_msg,
    mix_own, mix_send, mix_recv, in_own, in_send, in_recv,
    g_own, g_send, g_recv, h_own, h_send, h_recv,
    send_sem, recv_sem,
):
    seq, ch = lax.axis_index("seq"), lax.axis_index("ch")
    core, y, z = lax.rem(seq, 2), lax.rem(seq // 2, 4), seq // 8
    other = 1 - core

    def x_peer(k):
        return (seq, lax.rem(ch + k, 4))

    def zy_peer(dz, dy):
        return (lax.rem(z + dz, 4) * 8 + lax.rem(y + dy, 4) * 2 + core, ch)

    core_peer = (seq + 1 - 2 * core, ch)
    shifts = [(k // 4, k % 4) for k in range(1, PEERS)]

    def remote(src, dst, sem, device):
        return pltpu.make_async_remote_copy(
            src_ref=src,
            dst_ref=dst,
            send_sem=send_sem.at[sem],
            recv_sem=recv_sem.at[sem],
            device_id=device,
            device_id_type=MESH,
        )

    barrier = pltpu.get_barrier_semaphore()
    for device in (
        [x_peer(k) for k in range(1, 4)] + [core_peer] + [zy_peer(dz, dy) for dz, dy in shifts]
    ):
        pl.semaphore_signal(barrier, inc=1, device_id=device, device_id_type=MESH)
    pl.semaphore_wait(barrier, 3 + 1 + PEERS - 1)

    def cot_copy(k):
        return remote(cotangent, cot.at[ch], S_COT + k - 1, x_peer(k))

    for k in range(1, 4):
        cot_copy(k).start()
    cot[ch] = cotangent[...]

    anti = anti_identity()
    e = spread_matrix()
    for k in range(BLOCKS):
        here, there = slice(k * Q, (k + 1) * Q), slice(D - (k + 1) * Q, D - k * Q)
        px_flip[here, :] = mm(anti, proj_x[there, :]).astype(BF16)
        pz_flip[here, :] = mm(anti, proj_z[there, :]).astype(BF16)
        po_flip[:, here] = mm(proj_out[:, there], anti).astype(BF16)
        hidden_flip[:, here] = mm(hidden[:, there], anti).astype(BF16)
    small[...] = jnp.zeros_like(small)
    for weight, at in zip((proj_b, proj_c, proj_dt), range(3)):
        n = weight.shape[0]
        small[SMALL[0][at] : SMALL[0][at] + n, :] = weight[...]
        for k in range(BLOCKS):
            here, there = slice(k * Q, (k + 1) * Q), slice(D - (k + 1) * Q, D - k * Q)
            small[SMALL[1][at] : SMALL[1][at] + n, here] = mm(weight[:, there], anti).astype(BF16)

    def project_step(k, carry):
        rows = rows_of(k)
        u = hidden[rows, :]
        xs[0, rows, :] = mm(u, proj_x[...])
        zs[0, rows, :] = mm(u, proj_z[...])
        xs[1, rows, :] = mm(u, px_flip[...])
        zs[1, rows, :] = mm(u, pz_flip[...])
        narrow = mm_t(u, small[...])
        for strand in range(2):
            at_b, at_c, at_dt = SMALL[strand]
            bs[strand, rows, :] = narrow[:, at_b : at_b + NS].astype(BF16)
            cs[strand, rows, :] = narrow[:, at_c : at_c + NS].astype(BF16)
            dts[strand, rows, :] = narrow[:, at_dt : at_dt + HEADS] + bias[...]
        return carry

    lax.fori_loop(0, CHUNKS, project_step, 0)

    for k in range(1, 4):
        cot_copy(k).wait_recv()

    def cot_step(k, carry):
        rows = rows_of(k)
        forward = backward = None
        for b in range(BLOCKS):
            cot_flip[b, rows, :] = mm(cot[BLOCKS - 1 - b, rows, :], anti).astype(BF16)
            columns = slice(b * Q, (b + 1) * Q)
            part = mm_t(cot[b, rows, :], proj_out[:, columns])
            part_flip = mm_t(cot[b, rows, :], po_flip[:, columns])
            forward = part if forward is None else forward + part
            backward = part_flip if backward is None else backward + part_flip
        dos[0, rows, :] = forward.astype(BF16)
        dos[1, rows, :] = backward.astype(BF16)
        return carry

    lax.fori_loop(0, CHUNKS, cot_step, 0)

    def chunk_step(i, carry):
        strand, k = i // CHUNKS, lax.rem(i, CHUNKS)
        rows = rows_of(k)
        dt = softplus(dts[strand, rows, :])
        a = -rate[...] * dt
        cum = running(a, order(1 - 2 * strand))
        total = jnp.sum(a, axis=0, keepdims=True)
        cums[strand, rows, :] = cum
        dts_soft[strand, rows, :] = dt
        e_cum = spread(jnp.exp(cum), e)
        e_rest = spread(jnp.exp(total - cum), e)
        dt_wide = spread(dt, e)
        e_cums[strand, rows, :] = e_cum
        e_rests[strand, rows, :] = e_rest
        dt_wides[strand, rows, :] = dt_wide
        gate = zs[strand, rows, :]
        dy = dos[strand, rows, :].astype(F32) * (gate * sigmoid(gate))
        xd = xs[strand, rows, :] * dt_wide
        dyb[strand, rows, :] = dy.astype(BF16)
        xdt[strand, rows, :] = xd.astype(BF16)
        chunk_state[strand, k] = t_mm(bs[strand, rows, :], (xd * e_rest).astype(BF16))
        chunk_grad[strand, k] = t_mm(cs[strand, rows, :], (dy * e_cum).astype(BF16))
        chunk_decay[strand, k] = jnp.broadcast_to(jnp.exp(spread(total, e)), (8, W))
        return carry

    lax.fori_loop(0, 2 * CHUNKS, chunk_step, 0)

    for strand in range(2):
        times = list(range(CHUNKS)) if strand == 0 else list(range(CHUNKS))[::-1]
        state = chunk_state[strand, times[0]]
        grad = chunk_grad[strand, times[-1]]
        decay = chunk_decay[strand, 0]
        for k in times[1:]:
            state = chunk_decay[strand, k, 0:1, :] * state + chunk_state[strand, k]
        for k in times[::-1][1:]:
            grad = chunk_decay[strand, k, 0:1, :] * grad + chunk_grad[strand, k]
        for k in range(1, CHUNKS):
            decay = decay * chunk_decay[strand, k]
        at = 32 * strand
        msg[at : at + NS, :] = state
        msg[48 - at : 48 - at + NS, :] = grad
        if strand == 0:
            decay_f = decay
        else:
            msg[64:72, :] = jnp.where(iota((8, W), 0) == 0, decay_f, decay)

    def pieces(ref):
        return (
            ref[0:16, :], ref[16:32, :], ref[32:48, :], ref[48:64, :], ref[64:65, :], ref[65:66, :]
        )

    def rising(acc, part):
        return acc[0] * part[4] + part[0], acc[1] * part[5] + part[1]

    def falling(acc, part):
        return acc[0] * part[5] + part[2], acc[1] * part[4] + part[3]

    def pick(flag, new, old):
        return tuple(jnp.where(flag, n, o) for n, o in zip(new, old))

    def store_message(dst, up, down, decay_f, decay_r):
        dst[0:16, :], dst[16:32, :] = up
        dst[32:48, :], dst[48:64, :] = down
        dst[64:72, :] = jnp.where(
            iota((8, W), 0) == 0,
            jnp.broadcast_to(decay_f, (8, W)),
            jnp.broadcast_to(decay_r, (8, W)),
        )

    zero = jnp.zeros((NS, W), F32)

    def core_copy():
        return remote(msg, msg_core, S_CORE, core_peer)

    def y_copy(k):
        return remote(pair_msg, ybuf.at[y], S_Y + k - 1, zy_peer(0, k))

    def z_copy(k):
        return remote(y_msg, zbuf.at[z], S_Z + k - 1, zy_peer(k, 0))

    core_copy().start()

    def pair_stage():
        core_copy().wait_recv()
        mine, theirs = pieces(msg), pieces(msg_core)
        first, second = pick(core == 0, mine, theirs), pick(core == 0, theirs, mine)
        up = rising(first[:2], second)
        down = falling(second[2:4], first)
        decay_f, decay_r = first[4] * second[4], first[5] * second[5]
        store_message(pair_msg, up, down, decay_f, decay_r)
        store_message(ybuf.at[y], up, down, decay_f, decay_r)
        for k in range(1, 4):
            y_copy(k).start()

    def y_stage():
        for k in range(1, 4):
            y_copy(k).wait_recv()
        up = down = (zero, zero)
        decay_f = decay_r = jnp.ones((1, W), F32)
        for j in range(4):
            part = pieces(ybuf.at[j])
            up = rising(up, part)
            down = falling(down, pieces(ybuf.at[3 - j]))
            decay_f, decay_r = decay_f * part[4], decay_r * part[5]
        store_message(y_msg, up, down, decay_f, decay_r)
        store_message(zbuf.at[z], up, down, decay_f, decay_r)
        for k in range(1, 4):
            z_copy(k).start()

    def inner_step(i, carry):
        strand, k = i // CHUNKS, lax.rem(i, CHUNKS)
        rows = rows_of(k)
        mask = order(1 - 2 * strand)
        cum = cums[strand, rows, :]
        cum_t = cum.T
        b = bs[strand, rows, :]
        c = cs[strand, rows, :]
        scores = mm_t(c, b)
        lane = iota((Q, 128), 1)
        for pair in range(HEADS // 2):
            columns = slice(pair * 128, (pair + 1) * 128)
            x_pair, dy_pair = xdt[strand, rows, columns], dyb[strand, rows, columns]
            y_sum = g_sum = None
            for half in range(2):
                h = 2 * pair + half
                own = (lane >= HEAD) if half else (lane < HEAD)
                x_own = jnp.where(own, x_pair, jnp.zeros((), BF16))
                dy_own = jnp.where(own, dy_pair, jnp.zeros((), BF16))
                decay = jnp.exp(
                    jnp.where(mask, cum[:, h : h + 1] - cum_t[h : h + 1, :], -1e30)
                )
                cross = mm_t(dy_own, x_pair)
                mixing = (decay * scores).astype(BF16)
                if h == 0:
                    zacc[...] = decay * cross
                else:
                    zacc[...] += decay * cross
                y_new, g_new = mm(mixing, x_own), t_mm(mixing, dy_own)
                y_sum, g_sum = (
                    (y_new, g_new) if y_sum is None else (y_sum + y_new, g_sum + g_new)
                )
            yi[strand, rows, columns] = y_sum
            gi[strand, rows, columns] = g_sum
        both = zacc[...].astype(BF16)
        dcs[strand, rows, :] = mm(both, b)
        dbs[strand, rows, :] = t_mm(both, c)

        @pl.when(i == 0)
        def _():
            pair_stage()

        @pl.when(i == 1)
        def _():
            y_stage()

        return carry

    lax.fori_loop(0, 2 * CHUNKS, inner_step, 0)

    for k in range(1, 4):
        z_copy(k).wait_recv()
    up = down = (zero, zero)
    for buffer, at in ((zbuf, z), (ybuf, y)):
        for j in range(4):
            up = pick(j < at, rising(up, pieces(buffer.at[j])), up)
            down = pick(3 - j > at, falling(down, pieces(buffer.at[3 - j])), down)
    theirs = pieces(msg_core)
    up = pick(core == 1, rising(up, theirs), up)
    down = pick(core == 0, falling(down, theirs), down)

    for strand, (state, grad) in enumerate(((up[0], down[1]), (down[0], up[1]))):
        times = list(range(CHUNKS)) if strand == 0 else list(range(CHUNKS))[::-1]
        entering, leaving, leaving_grad = {}, {}, {}
        for k in times:
            entering[k] = state
            state = chunk_decay[strand, k, 0:1, :] * state + chunk_state[strand, k]
            leaving[k] = state
        for k in times[::-1]:
            leaving_grad[k] = grad
            grad = chunk_decay[strand, k, 0:1, :] * grad + chunk_grad[strand, k]
        for k in range(CHUNKS):
            chunk_state[strand, k] = entering[k]
            chunk_grad[strand, k] = leaving_grad[k]
            chunk_dot[strand, k] = jnp.broadcast_to(
                jnp.sum(leaving[k] * leaving_grad[k], axis=0, keepdims=True), (8, W)
            )

    skip_wide = spread(skip[...], e)
    ext[...] = jnp.zeros_like(ext)

    def mix_copy(k, j):
        rows = rows_of(k)
        return remote(
            mix_send.at[lax.rem(ch + j, 4), rows], mix_recv.at[j - 1, rows],
            S_MIX + 3 * k + j - 1, x_peer(j),
        )

    def in_copy(k, j):
        rows = rows_of(k)
        return remote(
            in_send.at[lax.rem(ch + j, 4), rows], in_recv.at[j - 1, rows],
            S_IN + 3 * k + j - 1, x_peer(j),
        )

    def keep(own, b, rows, part):
        @pl.when(ch == b)
        def _():
            own[rows, :] = part

    def outer_step(k, carry):
        rows = rows_of(k)
        for strand in range(2):
            raw = dts[strand, rows, :]
            dt = dts_soft[strand, rows, :]
            e_cum = e_cums[strand, rows, :]
            e_rest = e_rests[strand, rows, :]
            dt_wide = dt_wides[strand, rows, :]
            state = chunk_state[strand, k].astype(BF16)
            grad = chunk_grad[strand, k].astype(BF16)
            x = xs[strand, rows, :]
            gate = zs[strand, rows, :]
            d_o = dos[strand, rows, :].astype(F32)
            sig = sigmoid(gate)
            silu = gate * sig
            dy = d_o * silu
            y_part = yi[strand, rows, :] + e_cum * mm(cs[strand, rows, :], state)
            gb = gi[strand, rows, :] + e_rest * mm(bs[strand, rows, :], grad)
            out = y_part + skip_wide * x
            os[strand, rows, :] = (out * silu).astype(BF16)
            dzs[strand, rows, :] = (d_o * out * (sig + silu * (1.0 - sig))).astype(BF16)
            dxs[strand, rows, :] = (dt_wide * gb + skip_wide * dy).astype(BF16)
            d_c = dcs[strand, rows, :] + mm_t((dy * e_cum).astype(BF16), state)
            d_b = dbs[strand, rows, :] + mm_t((x * dt_wide * e_rest).astype(BF16), grad)
            direct = gather_heads(x * gb, e)
            d_cum = gather_heads(dy * y_part, e) - dt * direct
            d_a = running(d_cum, order(2 * strand - 1)) + gather_heads(chunk_dot[strand, k], e)[0:1, :]
            d_raw = (direct - rate[...] * d_a) * sigmoid(raw)
            at_b, at_c, at_dt = SMALL[strand]
            ext[rows, at_b : at_b + NS] = d_b.astype(BF16)
            ext[rows, at_c : at_c + NS] = d_c.astype(BF16)
            ext[rows, at_dt : at_dt + HEADS] = d_raw.astype(BF16)
        for b in range(BLOCKS):
            columns = slice(b * Q, (b + 1) * Q)
            part = mm(os[0, rows, :], proj_out[:, columns]) + mm(os[1, rows, :], po_flip[:, columns])
            keep(mix_own, b, rows, part)
            mix_send[b, rows, :] = part.astype(BF16)
        for j in range(1, 4):
            mix_copy(k, j).start()
        for b in range(BLOCKS):
            columns = slice(b * Q, (b + 1) * Q)
            part = (
                mm_t(dxs[0, rows, :], proj_x[columns, :])
                + mm_t(dzs[0, rows, :], proj_z[columns, :])
                + mm_t(dxs[1, rows, :], px_flip[columns, :])
                + mm_t(dzs[1, rows, :], pz_flip[columns, :])
                + mm(ext[rows, :], small[:, columns])
            )
            keep(in_own, b, rows, part)
            in_send[b, rows, :] = part.astype(BF16)
        for j in range(1, 4):
            in_copy(k, j).start()
        return carry

    lax.fori_loop(0, CHUNKS, outer_step, 0)

    def g_core_copy(n):
        return remote(g_send.at[n, :, other], g_recv.at[n], S_GCORE + n, core_peer)

    def g_peer_copy(n, dz, dy):
        to = lax.rem(z + dz, 4) * 4 + lax.rem(y + dy, 4)
        at = 4 * dz + dy
        return remote(
            h_send.at[n, to], h_recv.at[n, at], S_GPEER + PEERS * n + at, zy_peer(dz, dy)
        )

    def weight_part(n, left, left_flip, right):
        def step(b, carry):
            value = t_mm(left(b), right[0]) + t_mm(left_flip(b), right[1])
            g_own[n, pl.ds(pl.multiple_of(b * 4, 4), 4)] = value.reshape(4, 2, ROWS, W)
            g_send[n, pl.ds(pl.multiple_of(b * 4, 4), 4)] = value.astype(BF16).reshape(
                4, 2, ROWS, W
            )
            return carry

        lax.fori_loop(0, BLOCKS, step, 0)
        g_core_copy(n).start()

    weight_part(0, lambda b: cot[b], lambda b: cot_flip[b], os)
    weight_part(1, lambda b: hidden[:, rows_of(b)], lambda b: hidden_flip[:, rows_of(b)], dzs)
    weight_part(2, lambda b: hidden[:, rows_of(b)], lambda b: hidden_flip[:, rows_of(b)], dxs)

    for n in range(3):
        g_core_copy(n).wait_recv()

        def pair_sum(i, carry):
            value = g_own[n, i, core] + g_recv[n, i].astype(F32)
            h_send[n, i] = value.astype(BF16)
            return carry

        lax.fori_loop(0, PEERS, pair_sum, 0)
        at = z * 4 + y
        h_own[n] = g_own[n, at, core] + g_recv[n, at].astype(F32)
        for dz, dy in shifts:
            g_peer_copy(n, dz, dy).start()

    def finish_step(k, carry):
        rows = rows_of(k)
        for j in range(1, 4):
            mix_copy(k, j).wait_recv()
        mine = hidden[rows, pl.ds(pl.multiple_of(ch * Q, Q), Q)].astype(F32)
        total = mine + mix_own[rows, :]
        for j in range(3):
            total = total + mix_recv[j, rows, :].astype(F32)
        block_out[rows, :] = total.astype(BF16)
        for j in range(1, 4):
            in_copy(k, j).wait_recv()
        total = cotangent[rows, :].astype(F32) + in_own[rows, :]
        for j in range(3):
            total = total + in_recv[j, rows, :].astype(F32)
        grad_hidden[rows, :] = total
        return carry

    lax.fori_loop(0, CHUNKS, finish_step, 0)

    for n, out in enumerate((grad_out, grad_z, grad_x)):
        total = h_own[n]
        for dz, dy in shifts:
            g_peer_copy(n, dz, dy).wait_recv()
            total = total + h_recv[n, 4 * dz + dy].astype(F32)
        out[...] = total

    for k in range(1, 4):
        cot_copy(k).wait_send()
        y_copy(k).wait_send()
        z_copy(k).wait_send()
    core_copy().wait_send()
    for k in range(CHUNKS):
        for j in range(1, 4):
            mix_copy(k, j).wait_send()
            in_copy(k, j).wait_send()
    for n in range(3):
        g_core_copy(n).wait_send()
        for dz, dy in shifts:
            g_peer_copy(n, dz, dy).wait_send()


def shape(*dims, dtype=F32):
    return jax.ShapeDtypeStruct(dims, dtype)


VMEM = pl.BlockSpec(memory_space=pltpu.VMEM)


def body(
    hidden, proj_x, proj_z, proj_b, proj_c, proj_dt, dt_bias, decay_rate, skip_gain, proj_out, cotangent
):
    bias, rate, skip = (v[None, :] for v in (dt_bias, decay_rate, skip_gain))
    vm = pltpu.VMEM
    block_out, grad_hidden, grad_x, grad_z, grad_out = pl.pallas_call(
        block_kernel,
        out_shape=(
            shape(L, Q, dtype=BF16),
            shape(L, Q),
            shape(ROWS, W),
            shape(ROWS, W),
            shape(ROWS, W),
        ),
        in_specs=[VMEM] * 11,
        out_specs=[VMEM] * 5,
        scratch_shapes=[
            vm((D, W), BF16), vm((D, W), BF16), vm((W, D), BF16), vm((128, D), BF16),
            vm((L, D), BF16), vm((BLOCKS, L, Q), BF16), vm((BLOCKS, L, Q), BF16),
            vm((2, L, W), F32), vm((2, L, W), F32), vm((2, L, NS), BF16), vm((2, L, NS), BF16),
            vm((2, L, HEADS), F32), vm((2, L, W), BF16), vm((2, L, HEADS), F32),
            vm((2, L, HEADS), F32), vm((2, L, W), F32), vm((2, L, W), F32), vm((2, L, W), F32),
            vm((2, L, W), BF16), vm((2, L, W), BF16), vm((Q, Q), F32),
            vm((2, L, W), F32), vm((2, L, W), F32), vm((2, L, NS), F32), vm((2, L, NS), F32),
            vm((L, 128), BF16), vm((2, L, W), BF16), vm((2, L, W), BF16), vm((2, L, W), BF16),
            vm((2, CHUNKS, NS, W), F32), vm((2, CHUNKS, NS, W), F32),
            vm((2, CHUNKS, 8, W), F32), vm((2, CHUNKS, 8, W), F32),
            vm((72, W), F32), vm((72, W), F32), vm((4, 72, W), F32), vm((4, 72, W), F32),
            vm((72, W), F32), vm((72, W), F32),
            vm((L, Q), F32), vm((BLOCKS, L, Q), BF16), vm((3, L, Q), BF16),
            vm((L, Q), F32), vm((BLOCKS, L, Q), BF16), vm((3, L, Q), BF16),
            vm((3, PEERS, 2, ROWS, W), F32), vm((3, PEERS, 2, ROWS, W), BF16),
            vm((3, PEERS, ROWS, W), BF16),
            vm((3, ROWS, W), F32), vm((3, PEERS, ROWS, W), BF16),
            vm((3, PEERS, ROWS, W), BF16),
            pltpu.SemaphoreType.DMA((S_ALL,)), pltpu.SemaphoreType.DMA((S_ALL,)),
        ],
        compiler_params=pltpu.CompilerParams(
            vmem_limit_bytes=60 * 2**20, collective_id=0, has_side_effects=True
        ),
        name="block",
    )(
        hidden, proj_x, proj_z, proj_b.T, proj_c.T, proj_dt.T, bias, rate, skip, proj_out, cotangent
    )
    return block_out, grad_hidden, grad_x, grad_z, grad_out.T


def solution(mesh):
    return jax.shard_map(
        body,
        mesh=mesh,
        in_specs=(
            P("seq", None),
            P(None, "ch"),
            P(None, "ch"),
            P(),
            P(),
            P(None, "ch"),
            P("ch"),
            P("ch"),
            P("ch"),
            P("ch", None),
            P("seq", "ch"),
        ),
        out_specs=(P("seq", "ch"), P("seq", "ch"), P("seq", "ch"), P("seq", "ch"), P("ch", "seq")),
        check_vma=False,
    )
```

time: 423 us -> 97.4 us (0.23)
  waiting for transfers between devices: 340 us -> 0 us
  Pallas kernels: 56.8 us -> 91.5 us
  between operations: 14.1 us -> 0.66 us
    reduce_scatter x4 -> x0, waiting for transfers between devices: 220 us -> none  [the longest x1 81.9 us: body(): both = lax.psum_scatter(grad_w, 'seq', scatter_dimension=0, tiled=True)]
    all_gather x3 -> x0, waiting for transfers between devices: 117 us -> none  [the longest x1 47.9 us: body(): states = lax.all_gather(state, 'seq')]
    pallas_call x2 -> x1, Pallas kernels: 56.8 us -> 91.5 us  [body(): pl.pallas_call(block_kernel, out_shape=(shape(L, Q, dtype=BF16), shape(L,...]
  transfers between devices with their start and end apart: 7 -> 0, of which waited for: 7 -> 0; matrix products, arithmetic and copies ran while one was open for 2% -> 0% of each run, Pallas kernels for 0% -> 0%
where the time goes in v1:
time: 97.4 us; the launch traced here: 97.1 us
  Pallas kernels  91.5 us (94%)
  local copies, waits for them, and re-layouts  4.95 us (5%)
    pallas_call x1, Pallas kernels, body(): pl.pallas_call(block_kernel, out_shape=(shape(L, Q, dtype=BF16), shape(L,...  91.5 us
    unnamed x13, local copies, waits for them, and re-layouts  4.95 us

profile of v1, /device:TPU:1, one launch (start us, length us, event | category | flops | bytes accessed | tf_op | source)
XLA Modules:
  0.0 97.1 jit_solution(12048238104467095264)
XLA Ops:
  0.6 91.5 %block.1 = (bf16[512,256]{1,0:T(8,128)(2,1)}, f32[512,256]{1,0:T(8,128)}, f32[32,512]{1,0:T(8,128)}, f32[32,512]{1,0:T(8,128)}, f32[32,512]{1,0:T(8,128)}) custom-call(bf16[512,1024]{1,0:T(8,128)(2,1)} %hidden.1, bf16[1024,512]{1,0:T(8,128)(2,1)} %proj_x.1, bf16[1024,512]{1,0:T(8,128)(2,1)} %proj_z.1, bf16[16,1024]{1,0:T(8,128)(2,1)} %bitcast.8, ...), custom_call_target="tpu_custom_call" | custom-call | tf_op jit(solution)/shard_map/block/pallas_call | solution.py:559
  92.1 0.0 copy-start
  92.1 1.7 %copy.21 = bf16[512,256]{1,0:T(8,128)(2,1)} copy(bf16[512,256]{1,0:T(8,128)(2,1)} %get-tuple-element.20) | data formatting | bytes 524288
  93.8 0.0 copy-done
  93.8 0.0 copy-start.3
  93.8 0.8 copy.22
  94.6 0.1 copy-done.3
  94.7 0.0 copy-start.2
  94.7 0.6 copy.23
  95.3 0.2 copy-done.2
  95.6 0.0 copy-start.1
  95.6 0.6 copy.24
  96.2 0.2 copy-done.1
  96.4 0.6 copy.25
Async XLA Ops:
  92.1 1.7 %copy-start = (f32[512,256]{1,0:T(8,128)S(1)}, f32[512,256]{1,0:T(8,128)}, u32[]{:S(2)}) copy-start(f32[512,256]{1,0:T(8,128)} %get-tuple-element.21) | copy-start | bytes 1572868
  93.8 0.9 copy-start.3
  94.7 0.9 copy-start.2
  95.6 0.9 copy-start.1

commit v2 on v1

v2 whole, which is shorter than its diff:
```python
import jax
import jax.numpy as jnp
from jax import lax
from jax.experimental import pallas as pl
from jax.experimental.pallas import tpu as pltpu
from jax.sharding import PartitionSpec as P

L = 512
D = 1024
W = 512
HEADS = 8
HEAD = 64
NS = 16
Q = 256
CHUNKS = L // Q
BLOCKS = D // Q
PEERS = 16
ROWS = 32
F32 = jnp.float32
BF16 = jnp.bfloat16
MESH = pl.DeviceIdType.MESH

LAST = (((1,), (1,)), ((), ()))
FIRST = (((0,), (0,)), ((), ()))

SMALL = ((0, 16, 32), (48, 64, 80))

S_COT, S_MIX, S_IN, S_A, S_B = 0, 6, 12, 18, 36
S_GCORE, S_GPEER = 54, 57
S_ALL = S_GPEER + 3 * 16


def mm(a, b):
    return jnp.dot(a, b, preferred_element_type=F32)


def mm_t(a, b):
    return lax.dot_general(a, b, LAST, preferred_element_type=F32)


def t_mm(a, b):
    return lax.dot_general(a, b, FIRST, preferred_element_type=F32)


def split2(v):
    high = v.astype(BF16)
    return high, (v - high.astype(F32)).astype(BF16)


def split3(v):
    high = v.astype(BF16)
    rest = v - high.astype(F32)
    mid = rest.astype(BF16)
    return high, mid, (rest - mid.astype(F32)).astype(BF16)


def iota(shape, dim):
    return lax.broadcasted_iota(jnp.int32, shape, dim)


def anti_identity():
    return jnp.where(iota((Q, Q), 0) + iota((Q, Q), 1) == Q - 1, 1.0, 0.0).astype(BF16)


def spread_matrix():
    return jnp.where(iota((HEADS, W), 1) // HEAD == iota((HEADS, W), 0), 1.0, 0.0).astype(BF16)


def spread(v, e):
    high, low = split2(v)
    return mm(high, e) + mm(low, e)


def gather_heads(v, e):
    high, low = split2(v)
    return mm_t(high, e) + mm_t(low, e)


def order(sign):
    return (iota((Q, Q), 0) - iota((Q, Q), 1)) * sign >= 0


def running(v, mask):
    ones = jnp.where(mask, 1.0, 0.0).astype(BF16)
    return sum(mm(ones, part) for part in split3(v))


def softplus(v):
    return jnp.maximum(v, 0.0) + jnp.log1p(jnp.exp(-jnp.abs(v)))


def sigmoid(v):
    return 1.0 / (1.0 + jnp.exp(-v))


def rows_of(k):
    return pl.ds(pl.multiple_of(k * Q, Q), Q)


def block_kernel(
    hidden_hbm, proj_x_hbm, proj_z_hbm, proj_out_hbm, cot_hbm,
    proj_b, proj_c, proj_dt, bias, rate, skip,
    block_out, grad_hidden, grad_x, grad_z, grad_out,
    hidden, proj_x, proj_z, proj_out,
    px_flip, pz_flip, po_flip, small, hidden_flip, cot, cot_flip,
    xs, zs, bs, cs, dts, dos, cums, dts_soft, e_cums, e_rests, dt_wides, dyb, xdt, zacc,
    yi, gi, dcs, dbs, dyy, ext, os, dxs, dzs,
    chunk_state, chunk_grad, chunk_decay, chunk_dot,
    a_msg, a_core, a_pair, a_slots, a_back, a_in,
    b_msg, b_core, b_pair, b_slots, b_back, b_in,
    mix_own, mix_part, mix_send, mix_fwd, mix_recv,
    in_own, in_part, in_send, in_fwd, in_recv,
    g_own, g_send, g_recv, h_own, h_send, h_recv,
    load_sem, send_sem, recv_sem,
):
    seq, ch = lax.axis_index("seq"), lax.axis_index("ch")
    core, y, z = lax.rem(seq, 2), lax.rem(seq // 2, 4), seq // 8
    other = 1 - core
    place = z * 4 + y

    def x_peer(k):
        return (seq, lax.rem(ch + k, 4))

    def zy_peer(dz, dy):
        return (lax.rem(z + dz, 4) * 8 + lax.rem(y + dy, 4) * 2 + core, ch)

    core_peer = (seq + 1 - 2 * core, ch)
    shifts = [(k // 4, k % 4) for k in range(1, PEERS)]

    def remote(src, dst, sem, device):
        return pltpu.make_async_remote_copy(
            src_ref=src,
            dst_ref=dst,
            send_sem=send_sem.at[sem],
            recv_sem=recv_sem.at[sem],
            device_id=device,
            device_id_type=MESH,
        )

    barrier = pltpu.get_barrier_semaphore()
    for device in [x_peer(1), x_peer(3), core_peer] + [zy_peer(dz, dy) for dz, dy in shifts]:
        pl.semaphore_signal(barrier, inc=1, device_id=device, device_id_type=MESH)

    loads = [
        pltpu.make_async_copy(src, dst, load_sem.at[n])
        for n, (src, dst) in enumerate(
            (
                (cot_hbm, cot.at[ch]),
                (hidden_hbm, hidden),
                (proj_x_hbm, proj_x),
                (proj_z_hbm, proj_z),
                (proj_out_hbm, proj_out),
            )
        )
    ]
    for load in loads:
        load.start()
    anti = anti_identity()
    e = spread_matrix()
    small[...] = jnp.zeros_like(small)
    for weight, at in zip((proj_b, proj_c, proj_dt), range(3)):
        n = weight.shape[0]
        small[SMALL[0][at] : SMALL[0][at] + n, :] = weight[...]
        for k in range(BLOCKS):
            here, there = slice(k * Q, (k + 1) * Q), slice(D - (k + 1) * Q, D - k * Q)
            small[SMALL[1][at] : SMALL[1][at] + n, here] = mm(weight[:, there], anti).astype(BF16)
    loads[0].wait()
    pl.semaphore_wait(barrier, 2 + 1 + PEERS - 1)

    half = [slice(0, Q), slice(Q, L)]
    before, after = lax.rem(ch + 3, 4), lax.rem(ch + 1, 4)

    def cot_copy(n):
        block, rows, to = (
            (ch, half[0], 1), (ch, half[1], 3), (ch, half[1], 1), (ch, half[0], 3),
            (before, half[0], 1), (after, half[1], 3),
        )[n]
        return remote(cot.at[block, rows], cot.at[block, rows], S_COT + n, x_peer(to))

    for n in range(4):
        cot_copy(n).start()

    loads[1].wait()
    loads[2].wait()
    loads[3].wait()
    for k in range(BLOCKS):
        here, there = slice(k * Q, (k + 1) * Q), slice(D - (k + 1) * Q, D - k * Q)
        px_flip[here, :] = mm(anti, proj_x[there, :]).astype(BF16)
        pz_flip[here, :] = mm(anti, proj_z[there, :]).astype(BF16)
        hidden_flip[:, here] = mm(hidden[:, there], anti).astype(BF16)

    def project_step(k, carry):
        rows = rows_of(k)
        u = hidden[rows, :]
        xs[0, rows, :] = mm(u, proj_x[...])
        zs[0, rows, :] = mm(u, proj_z[...])
        xs[1, rows, :] = mm(u, px_flip[...])
        zs[1, rows, :] = mm(u, pz_flip[...])
        narrow = mm_t(u, small[...])
        for strand in range(2):
            at_b, at_c, at_dt = SMALL[strand]
            bs[strand, rows, :] = narrow[:, at_b : at_b + NS].astype(BF16)
            cs[strand, rows, :] = narrow[:, at_c : at_c + NS].astype(BF16)
            dts[strand, rows, :] = narrow[:, at_dt : at_dt + HEADS] + bias[...]
        return carry

    lax.fori_loop(0, CHUNKS, project_step, 0)

    for n in range(2):
        cot_copy(n).wait_recv()
        cot_copy(4 + n).start()

    def state_step(i, carry):
        strand, k = i // CHUNKS, lax.rem(i, CHUNKS)
        rows = rows_of(k)
        dt = softplus(dts[strand, rows, :])
        a = -rate[...] * dt
        cum = running(a, order(1 - 2 * strand))
        total = jnp.sum(a, axis=0, keepdims=True)
        cums[strand, rows, :] = cum
        dts_soft[strand, rows, :] = dt
        e_rest = spread(jnp.exp(total - cum), e)
        dt_wide = spread(dt, e)
        e_cums[strand, rows, :] = spread(jnp.exp(cum), e)
        e_rests[strand, rows, :] = e_rest
        dt_wides[strand, rows, :] = dt_wide
        xd = xs[strand, rows, :] * dt_wide
        xdt[strand, rows, :] = xd.astype(BF16)
        chunk_state[strand, k] = t_mm(bs[strand, rows, :], (xd * e_rest).astype(BF16))
        chunk_decay[strand, k] = jnp.broadcast_to(jnp.exp(spread(total, e)), (8, W))
        return carry

    lax.fori_loop(0, 2 * CHUNKS, state_step, 0)

    def times(strand):
        return list(range(CHUNKS)) if strand == 0 else list(range(CHUNKS))[::-1]

    def two_halves(dst, rows, value):
        dst[0, rows, :] = value[:, 0:Q]
        dst[1, rows, :] = value[:, Q:]

    decays = []
    for strand in range(2):
        state, decay = chunk_state[strand, times(strand)[0]], chunk_decay[strand, 0]
        for k in times(strand)[1:]:
            state = chunk_decay[strand, k, 0:1, :] * state + chunk_state[strand, k]
        for k in range(1, CHUNKS):
            decay = decay * chunk_decay[strand, k]
        two_halves(a_msg, slice(16 * strand, 16 * strand + NS), state)
        decays.append(decay)
    two_halves(a_msg, slice(32, 40), jnp.where(iota((8, W), 0) == 0, decays[0], decays[1]))

    zero = jnp.zeros((NS, Q), F32)
    a_slots[place] = jnp.zeros_like(a_slots[0])
    b_slots[place] = jnp.zeros_like(b_slots[0])

    class Exchange:
        def __init__(self, base, msg, from_core, pair, slots, back, result, swap):
            self.base, self.msg, self.from_core, self.pair = base, msg, from_core, pair
            self.slots, self.back, self.result, self.swap = slots, back, result, swap

        def to_core(self):
            return remote(self.msg.at[other], self.from_core, self.base, core_peer)

        def to_place(self, dz, dy):
            to = lax.rem(z + dz, 4) * 4 + lax.rem(y + dy, 4)
            kind = jnp.where(to > place, 0, 1)
            return remote(
                self.pair.at[kind], self.slots.at[place], self.base + 4 * dz + dy, zy_peer(dz, dy)
            )

        def to_back(self):
            return remote(self.back, self.result.at[core], self.base + PEERS, core_peer)

        def decay(self, ref, strand):
            return ref[strand : strand + 1, :]

        def both(self):
            mine = (
                self.msg[core, 0:16, :], self.msg[core, 16:32, :],
                a_msg[core, 32 + self.swap : 33 + self.swap, :],
                a_msg[core, 33 - self.swap : 34 - self.swap, :],
            )
            theirs = (
                self.from_core[0:16, :], self.from_core[16:32, :],
                a_core[32 + self.swap : 33 + self.swap, :],
                a_core[33 - self.swap : 34 - self.swap, :],
            )
            return mine, theirs

        def spread_out(self):
            self.to_core().wait_recv()
            mine, theirs = self.both()
            first = [jnp.where(core == 0, m, t) for m, t in zip(mine, theirs)]
            second = [jnp.where(core == 0, t, m) for m, t in zip(mine, theirs)]
            up = second[2] * first[0] + second[0]
            down = first[3] * second[1] + first[1]
            self.pair[0, 0:16, :] = up
            self.pair[1, 0:16, :] = down
            if not self.swap:
                product = jnp.where(
                    iota((8, Q), 0) == 0,
                    jnp.broadcast_to(first[2] * second[2], (8, Q)),
                    jnp.broadcast_to(first[3] * second[3], (8, Q)),
                )
                self.pair[0, 16:24, :] = product
                self.pair[1, 16:24, :] = product
            for dz, dy in shifts:
                self.to_place(dz, dy).start()

        def collect(self):
            for dz, dy in shifts:
                self.to_place(dz, dy).wait_recv()
            up = down = zero
            for j in range(PEERS):
                r = PEERS - 1 - j
                decay_up = a_slots[j, 16 + self.swap : 17 + self.swap, :]
                decay_down = a_slots[r, 17 - self.swap : 18 - self.swap, :]
                up = jnp.where(j < place, decay_up * up + self.slots[j, 0:16, :], up)
                down = jnp.where(r > place, decay_down * down + self.slots[r, 0:16, :], down)
            mine, theirs = self.both()
            self.back[0:16, :] = jnp.where(core == 0, mine[2] * up + mine[0], up)
            self.back[16:32, :] = jnp.where(core == 1, mine[3] * down + mine[1], down)
            self.to_back().start()
            self.result[core, 0:16, :] = jnp.where(core == 1, theirs[2] * up + theirs[0], up)
            self.result[core, 16:32, :] = jnp.where(core == 0, theirs[3] * down + theirs[1], down)

        def take(self):
            self.to_back().wait_recv()
            return [
                jnp.concatenate([self.result[0, rows, :], self.result[1, rows, :]], axis=1)
                for rows in (slice(0, 16), slice(16, 32))
            ]

        def drain(self):
            self.to_core().wait_send()
            self.to_back().wait_send()
            for dz, dy in shifts:
                self.to_place(dz, dy).wait_send()

    round_a = Exchange(S_A, a_msg, a_core, a_pair, a_slots, a_back, a_in, 0)
    round_b = Exchange(S_B, b_msg, b_core, b_pair, b_slots, b_back, b_in, 1)
    round_a.to_core().start()

    lane = iota((Q, 128), 1)

    def within_step(i, carry):
        strand, k = i // CHUNKS, lax.rem(i, CHUNKS)
        rows = rows_of(k)
        mask = order(1 - 2 * strand)
        cum = cums[strand, rows, :]
        cum_t = cum.T
        scores = mm_t(cs[strand, rows, :], bs[strand, rows, :])
        for pair in range(HEADS // 2):
            columns = slice(pair * 128, (pair + 1) * 128)
            x_pair = xdt[strand, rows, columns]
            y_sum = None
            for odd in range(2):
                h = 2 * pair + odd
                own = (lane >= HEAD) if odd else (lane < HEAD)
                x_own = jnp.where(own, x_pair, jnp.zeros((), BF16))
                decay = jnp.exp(
                    jnp.where(mask, cum[:, h : h + 1] - cum_t[h : h + 1, :], -1e30)
                )
                y_new = mm((decay * scores).astype(BF16), x_own)
                y_sum = y_new if y_sum is None else y_sum + y_new
            yi[strand, rows, columns] = y_sum

        @pl.when(i == 0)
        def _():
            round_a.spread_out()

        return carry

    lax.fori_loop(0, 2 * CHUNKS, within_step, 0)

    loads[4].wait()
    for k in range(BLOCKS):
        here, there = slice(k * Q, (k + 1) * Q), slice(D - (k + 1) * Q, D - k * Q)
        po_flip[:, here] = mm(proj_out[:, there], anti).astype(BF16)
    round_a.collect()

    for n in range(2, 6):
        cot_copy(n).wait_recv()

    def cot_step(k, carry):
        rows = rows_of(k)
        forward = backward = None
        for b in range(BLOCKS):
            cot_flip[b, rows, :] = mm(cot[BLOCKS - 1 - b, rows, :], anti).astype(BF16)
            columns = slice(b * Q, (b + 1) * Q)
            part = mm_t(cot[b, rows, :], proj_out[:, columns])
            part_flip = mm_t(cot[b, rows, :], po_flip[:, columns])
            forward = part if forward is None else forward + part
            backward = part_flip if backward is None else backward + part_flip
        dos[0, rows, :] = forward.astype(BF16)
        dos[1, rows, :] = backward.astype(BF16)
        return carry

    lax.fori_loop(0, CHUNKS, cot_step, 0)

    def grad_step(i, carry):
        strand, k = i // CHUNKS, lax.rem(i, CHUNKS)
        rows = rows_of(k)
        gate = zs[strand, rows, :]
        dy = dos[strand, rows, :].astype(F32) * (gate * sigmoid(gate))
        dyb[strand, rows, :] = dy.astype(BF16)
        chunk_grad[strand, k] = t_mm(
            cs[strand, rows, :], (dy * e_cums[strand, rows, :]).astype(BF16)
        )
        return carry

    lax.fori_loop(0, 2 * CHUNKS, grad_step, 0)

    for strand in range(2):
        falling = times(strand)[::-1]
        grad = chunk_grad[strand, falling[0]]
        for k in falling[1:]:
            grad = chunk_decay[strand, k, 0:1, :] * grad + chunk_grad[strand, k]
        two_halves(b_msg, slice(16 - 16 * strand, 32 - 16 * strand), grad)
    round_b.to_core().start()

    for strand, state in enumerate(round_a.take()):
        for k in times(strand):
            own_state = chunk_state[strand, k]
            chunk_state[strand, k] = state
            state = chunk_decay[strand, k, 0:1, :] * state + own_state
            chunk_dot[strand, k] = state

    skip_wide = spread(skip[...], e)

    def out_step(i, carry):
        strand, k = i // CHUNKS, lax.rem(i, CHUNKS)
        rows = rows_of(k)
        e_cum = e_cums[strand, rows, :]
        state = chunk_state[strand, k].astype(BF16)
        gate = zs[strand, rows, :]
        d_o = dos[strand, rows, :].astype(F32)
        sig = sigmoid(gate)
        silu = gate * sig
        dy = d_o * silu
        y_part = yi[strand, rows, :] + e_cum * mm(cs[strand, rows, :], state)
        out = y_part + skip_wide * xs[strand, rows, :]
        os[strand, rows, :] = (out * silu).astype(BF16)
        dzs[strand, rows, :] = (d_o * out * (sig + silu * (1.0 - sig))).astype(BF16)
        dcs[strand, rows, :] = mm_t((dy * e_cum).astype(BF16), state)
        dyy[strand, rows, :] = gather_heads(dy * y_part, e)
        yi[strand, rows, :] = skip_wide * dy

        @pl.when(i == 1)
        def _():
            round_b.spread_out()

        return carry

    lax.fori_loop(0, 2 * CHUNKS, out_step, 0)

    class ColumnSum:
        def __init__(self, base, compute, own, part, send, forward, recv):
            self.base, self.compute, self.own, self.part = base, compute, own, part
            self.send, self.forward, self.recv = send, forward, recv

        def copy(self, n):
            src, dst, to = (
                (self.send.at[1, half[0]], self.forward.at[0], 1),
                (self.send.at[1, half[1]], self.forward.at[1], 3),
                (self.send.at[0, half[1]], self.recv.at[0, half[1]], 1),
                (self.send.at[2, half[0]], self.recv.at[1, half[0]], 3),
                (self.send.at[0, half[0]], self.recv.at[0, half[0]], 1),
                (self.send.at[2, half[1]], self.recv.at[1, half[1]], 3),
            )[n]
            return remote(src, dst, self.base + n, x_peer(to))

        def columns(self, r):
            return pl.ds(pl.multiple_of(lax.rem(ch + r, 4) * Q, Q), Q)

        def begin(self):
            for n in range(2):
                self.send[1, half[n], :] = self.compute(half[n], self.columns(2)).astype(BF16)
                self.copy(n).start()
            self.send[0, half[1], :] = self.compute(half[1], self.columns(1)).astype(BF16)
            self.copy(2).start()
            self.send[2, half[0], :] = self.compute(half[0], self.columns(3)).astype(BF16)
            self.copy(3).start()
            self.part[0] = self.compute(half[0], self.columns(1))
            self.part[1] = self.compute(half[1], self.columns(3))

        def middle(self):
            for n, block in ((0, 0), (1, 2)):
                self.copy(n).wait_recv()
                self.send[block, half[n], :] = (
                    self.part[n] + self.forward[n].astype(F32)
                ).astype(BF16)
                self.copy(4 + n).start()

        def own_block(self):
            for n in range(2):
                self.own[half[n], :] = self.compute(half[n], self.columns(0))

        def finish(self, rows):
            return (
                self.own[rows, :]
                + self.recv[0, rows, :].astype(F32)
                + self.recv[1, rows, :].astype(F32)
            )

        def arrived(self):
            for n in range(2, 6):
                self.copy(n).wait_recv()

        def drain(self):
            for n in range(6):
                self.copy(n).wait_send()

    def mix_block(rows, columns):
        return mm(os[0, rows, :], proj_out[:, columns]) + mm(os[1, rows, :], po_flip[:, columns])

    def in_block(rows, columns):
        return (
            mm_t(dxs[0, rows, :], proj_x[columns, :])
            + mm_t(dzs[0, rows, :], proj_z[columns, :])
            + mm_t(dxs[1, rows, :], px_flip[columns, :])
            + mm_t(dzs[1, rows, :], pz_flip[columns, :])
            + mm(ext[rows, :], small[:, columns])
        )

    mix_sum = ColumnSum(S_MIX, mix_block, mix_own, mix_part, mix_send, mix_fwd, mix_recv)
    in_sum = ColumnSum(S_IN, in_block, in_own, in_part, in_send, in_fwd, in_recv)
    mix_sum.begin()

    def inner_step(i, carry):
        strand, k = i // CHUNKS, lax.rem(i, CHUNKS)
        rows = rows_of(k)
        mask = order(2 * strand - 1)
        cum = cums[strand, rows, :]
        cum_t = cum.T
        b = bs[strand, rows, :]
        c = cs[strand, rows, :]
        scores = mm_t(b, c)
        for pair in range(HEADS // 2):
            columns = slice(pair * 128, (pair + 1) * 128)
            x_pair, dy_pair = xdt[strand, rows, columns], dyb[strand, rows, columns]
            g_sum = None
            for odd in range(2):
                h = 2 * pair + odd
                own = (lane >= HEAD) if odd else (lane < HEAD)
                dy_own = jnp.where(own, dy_pair, jnp.zeros((), BF16))
                decay = jnp.exp(
                    jnp.where(mask, cum_t[h : h + 1, :] - cum[:, h : h + 1], -1e30)
                )
                cross = mm_t(x_pair, dy_own)
                if h == 0:
                    zacc[...] = decay * cross
                else:
                    zacc[...] += decay * cross
                g_new = mm((decay * scores).astype(BF16), dy_own)
                g_sum = g_new if g_sum is None else g_sum + g_new
            gi[strand, rows, columns] = g_sum
        pairs = zacc[...].astype(BF16)
        dbs[strand, rows, :] = mm(pairs, c)
        dcs[strand, rows, :] += t_mm(pairs, b)

        @pl.when(i == 1)
        def _():
            mix_sum.middle()

        @pl.when(i == 2)
        def _():
            round_b.collect()

        return carry

    lax.fori_loop(0, 2 * CHUNKS, inner_step, 0)

    def g_core_copy(n):
        return remote(g_send.at[n, :, other], g_recv.at[n], S_GCORE + n, core_peer)

    def g_peer_copy(n, dz, dy):
        to = lax.rem(z + dz, 4) * 4 + lax.rem(y + dy, 4)
        at = 4 * dz + dy
        return remote(
            h_send.at[n, to], h_recv.at[n, at], S_GPEER + PEERS * n + at, zy_peer(dz, dy)
        )

    def weight_part(n, left, left_flip, right):
        def step(b, carry):
            value = t_mm(left(b), right[0]) + t_mm(left_flip(b), right[1])
            g_own[n, pl.ds(pl.multiple_of(b * 4, 4), 4)] = value.reshape(4, 2, ROWS, W)
            g_send[n, pl.ds(pl.multiple_of(b * 4, 4), 4)] = value.astype(BF16).reshape(
                4, 2, ROWS, W
            )
            return carry

        lax.fori_loop(0, BLOCKS, step, 0)
        g_core_copy(n).start()

    def weight_pair(n):
        g_core_copy(n).wait_recv()

        def pair_sum(i, carry):
            value = g_own[n, i, core] + g_recv[n, i].astype(F32)
            h_send[n, i] = value.astype(BF16)
            return carry

        lax.fori_loop(0, PEERS, pair_sum, 0)
        h_own[n] = g_own[n, place, core] + g_recv[n, place].astype(F32)
        for dz, dy in shifts:
            g_peer_copy(n, dz, dy).start()

    weight_part(0, lambda b: cot[b], lambda b: cot_flip[b], os)
    weight_part(1, lambda b: hidden[:, rows_of(b)], lambda b: hidden_flip[:, rows_of(b)], dzs)
    mix_sum.own_block()
    weight_pair(0)

    up, down = round_b.take()
    for strand, grad in enumerate((down, up)):
        for k in times(strand)[::-1]:
            own_grad = chunk_grad[strand, k]
            chunk_grad[strand, k] = grad
            chunk_dot[strand, k, 0:8, :] = jnp.broadcast_to(
                jnp.sum(grad * chunk_dot[strand, k], axis=0, keepdims=True), (8, W)
            )
            grad = chunk_decay[strand, k, 0:1, :] * grad + own_grad
    ext[...] = jnp.zeros_like(ext)

    def back_step(k, carry):
        rows = rows_of(k)
        for strand in range(2):
            dt = dts_soft[strand, rows, :]
            e_rest = e_rests[strand, rows, :]
            dt_wide = dt_wides[strand, rows, :]
            grad = chunk_grad[strand, k].astype(BF16)
            x = xs[strand, rows, :]
            gb = gi[strand, rows, :] + e_rest * mm(bs[strand, rows, :], grad)
            dxs[strand, rows, :] = (dt_wide * gb + yi[strand, rows, :]).astype(BF16)
            d_b = dbs[strand, rows, :] + mm_t((x * dt_wide * e_rest).astype(BF16), grad)
            direct = gather_heads(x * gb, e)
            d_cum = dyy[strand, rows, :] - dt * direct
            d_a = running(d_cum, order(2 * strand - 1)) + gather_heads(
                chunk_dot[strand, k, 0:8, :], e
            )[0:1, :]
            d_raw = (direct - rate[...] * d_a) * sigmoid(dts[strand, rows, :])
            at_b, at_c, at_dt = SMALL[strand]
            ext[rows, at_b : at_b + NS] = d_b.astype(BF16)
            ext[rows, at_c : at_c + NS] = dcs[strand, rows, :].astype(BF16)
            ext[rows, at_dt : at_dt + HEADS] = d_raw.astype(BF16)
        return carry

    lax.fori_loop(0, CHUNKS, back_step, 0)

    weight_part(2, lambda b: hidden[:, rows_of(b)], lambda b: hidden_flip[:, rows_of(b)], dxs)
    in_sum.begin()
    weight_pair(1)
    weight_pair(2)
    in_sum.middle()
    in_sum.own_block()

    mix_sum.arrived()

    def mix_step(k, carry):
        rows = rows_of(k)
        mine = hidden[rows, pl.ds(pl.multiple_of(ch * Q, Q), Q)].astype(F32)
        block_out[rows, :] = (mine + mix_sum.finish(rows)).astype(BF16)
        return carry

    lax.fori_loop(0, CHUNKS, mix_step, 0)
    in_sum.arrived()

    def in_step(k, carry):
        rows = rows_of(k)
        grad_hidden[rows, :] = cot[ch, rows, :].astype(F32) + in_sum.finish(rows)
        return carry

    lax.fori_loop(0, CHUNKS, in_step, 0)

    for n, out in enumerate((grad_out, grad_z, grad_x)):
        total = h_own[n]
        for dz, dy in shifts:
            g_peer_copy(n, dz, dy).wait_recv()
            total = total + h_recv[n, 4 * dz + dy].astype(F32)
        out[...] = total

    for n in range(6):
        cot_copy(n).wait_send()
    round_a.drain()
    round_b.drain()
    mix_sum.drain()
    in_sum.drain()
    for n in range(3):
        g_core_copy(n).wait_send()
        for dz, dy in shifts:
            g_peer_copy(n, dz, dy).wait_send()


def shape(*dims, dtype=F32):
    return jax.ShapeDtypeStruct(dims, dtype)


VMEM = pl.BlockSpec(memory_space=pltpu.VMEM)


def body(
    hidden, proj_x, proj_z, proj_b, proj_c, proj_dt, dt_bias, decay_rate, skip_gain, proj_out, cotangent
):
    bias, rate, skip = (v[None, :] for v in (dt_bias, decay_rate, skip_gain))
    vm = pltpu.VMEM
    block_out, grad_hidden, grad_x, grad_z, grad_out = pl.pallas_call(
        block_kernel,
        out_shape=(
            shape(L, Q, dtype=BF16),
            shape(L, Q),
            shape(ROWS, W),
            shape(ROWS, W),
            shape(ROWS, W),
        ),
        in_specs=[pl.BlockSpec(memory_space=pl.ANY)] * 5 + [VMEM] * 6,
        out_specs=[VMEM] * 5,
        scratch_shapes=[
            vm((L, D), BF16), vm((D, W), BF16), vm((D, W), BF16), vm((W, D), BF16),
            vm((D, W), BF16), vm((D, W), BF16), vm((W, D), BF16), vm((128, D), BF16),
            vm((L, D), BF16), vm((BLOCKS, L, Q), BF16), vm((BLOCKS, L, Q), BF16),
            vm((2, L, W), F32), vm((2, L, W), F32), vm((2, L, NS), BF16), vm((2, L, NS), BF16),
            vm((2, L, HEADS), F32), vm((2, L, W), BF16), vm((2, L, HEADS), F32),
            vm((2, L, HEADS), F32), vm((2, L, W), F32), vm((2, L, W), F32), vm((2, L, W), F32),
            vm((2, L, W), BF16), vm((2, L, W), BF16), vm((Q, Q), F32),
            vm((2, L, W), F32), vm((2, L, W), F32), vm((2, L, NS), F32), vm((2, L, NS), F32),
            vm((2, L, HEADS), F32),
            vm((L, 128), BF16), vm((2, L, W), BF16), vm((2, L, W), BF16), vm((2, L, W), BF16),
            vm((2, CHUNKS, NS, W), F32), vm((2, CHUNKS, NS, W), F32),
            vm((2, CHUNKS, 8, W), F32), vm((2, CHUNKS, NS, W), F32),
            vm((2, 40, Q), F32), vm((40, Q), F32), vm((2, 24, Q), F32), vm((PEERS, 24, Q), F32),
            vm((32, Q), F32), vm((2, 32, Q), F32),
            vm((2, 32, Q), F32), vm((32, Q), F32), vm((2, 16, Q), F32), vm((PEERS, 16, Q), F32),
            vm((32, Q), F32), vm((2, 32, Q), F32),
            vm((L, Q), F32), vm((2, Q, Q), F32), vm((3, L, Q), BF16), vm((2, Q, Q), BF16),
            vm((2, L, Q), BF16),
            vm((L, Q), F32), vm((2, Q, Q), F32), vm((3, L, Q), BF16), vm((2, Q, Q), BF16),
            vm((2, L, Q), BF16),
            vm((3, PEERS, 2, ROWS, W), F32), vm((3, PEERS, 2, ROWS, W), BF16),
            vm((3, PEERS, ROWS, W), BF16),
            vm((3, ROWS, W), F32), vm((3, PEERS, ROWS, W), BF16),
            vm((3, PEERS, ROWS, W), BF16),
            pltpu.SemaphoreType.DMA((5,)),
            pltpu.SemaphoreType.DMA((S_ALL,)), pltpu.SemaphoreType.DMA((S_ALL,)),
        ],
        compiler_params=pltpu.CompilerParams(
            vmem_limit_bytes=60 * 2**20, collective_id=0, has_side_effects=True
        ),
        name="block",
    )(
        hidden, proj_x, proj_z, proj_out, cotangent,
        proj_b.T, proj_c.T, proj_dt.T, bias, rate, skip,
    )
    return block_out, grad_hidden, grad_x, grad_z, grad_out.T


def solution(mesh):
    return jax.shard_map(
        body,
        mesh=mesh,
        in_specs=(
            P("seq", None),
            P(None, "ch"),
            P(None, "ch"),
            P(),
            P(),
            P(None, "ch"),
            P("ch"),
            P("ch"),
            P("ch"),
            P("ch", None),
            P("seq", "ch"),
        ),
        out_specs=(P("seq", "ch"), P("seq", "ch"), P("seq", "ch"), P("seq", "ch"), P("ch", "seq")),
        check_vma=False,
    )
```

time: 97.4 us -> 79.1 us (0.81)
  Pallas kernels: 91.5 us -> 72.4 us
    pallas_call x1, Pallas kernels: 91.5 us -> 72.4 us  [body(): pl.pallas_call(block_kernel, out_shape=(shape(L, Q, dtype=BF16), shape(L,...]
where the time goes in v2:
time: 79.1 us; the launch traced here: 78 us
  Pallas kernels  72.4 us (92%)
  local copies, waits for them, and re-layouts  4.95 us (6%)
    pallas_call x1, Pallas kernels, body(): pl.pallas_call(block_kernel, out_shape=(shape(L, Q, dtype=BF16), shape(L,...  72.4 us
    unnamed x13, local copies, waits for them, and re-layouts  4.95 us

profile of v2, /device:TPU:1, one launch (start us, length us, event | category | flops | bytes accessed | tf_op | source)
XLA Modules:
  0.0 78.0 jit_solution(4037018665284248548)
XLA Ops:
  0.6 72.4 %block.1 = (bf16[512,256]{1,0:T(8,128)(2,1)}, f32[512,256]{1,0:T(8,128)}, f32[32,512]{1,0:T(8,128)}, f32[32,512]{1,0:T(8,128)}, f32[32,512]{1,0:T(8,128)}) custom-call(bf16[512,1024]{1,0:T(8,128)(2,1)} %hidden_hbm.1, bf16[1024,512]{1,0:T(8,128)(2,1)} %proj_x_hbm.1, bf16[1024,512]{1,0:T(8,128)(2,1)} %proj_z_hbm.1, bf16[512,1024]{1,0:T(8,128)(2,1)} %proj_out_hbm.1, ...), custom_call_target="tpu_custom_call" | custom-call | tf_op jit(solution)/shard_map/block/pallas_call | solution.py:707
  73.1 0.0 copy-start
  73.1 1.7 %copy.21 = bf16[512,256]{1,0:T(8,128)(2,1)} copy(bf16[512,256]{1,0:T(8,128)(2,1)} %get-tuple-element.20) | data formatting | bytes 524288
  74.8 0.0 copy-done
  74.8 0.0 copy-start.3
  74.8 0.8 %copy.22 = f32[512,256]{1,0:T(8,128)} copy(f32[512,256]{1,0:T(8,128)S(1)} %copy-done) | data formatting | bytes 1048576
  75.6 0.1 copy-done.3
  75.7 0.0 copy-start.2
  75.7 0.6 copy.23
  76.3 0.2 copy-done.2
  76.5 0.0 copy-start.1
  76.5 0.6 copy.24
  77.2 0.2 copy-done.1
  77.4 0.6 copy.25
Async XLA Ops:
  73.1 1.7 %copy-start = (f32[512,256]{1,0:T(8,128)S(1)}, f32[512,256]{1,0:T(8,128)}, u32[]{:S(2)}) copy-start(f32[512,256]{1,0:T(8,128)} %get-tuple-element.21) | copy-start | bytes 1572868
  74.8 0.9 %copy-start.3 = (f32[32,512]{1,0:T(8,128)S(1)}, f32[32,512]{1,0:T(8,128)}, u32[]{:S(2)}) copy-start(f32[32,512]{1,0:T(8,128)} %get-tuple-element.22) | copy-start | bytes 196612
  75.7 0.9 %copy-start.2 = (f32[32,512]{1,0:T(8,128)S(1)}, f32[32,512]{1,0:T(8,128)}, u32[]{:S(2)}) copy-start(f32[32,512]{1,0:T(8,128)} %get-tuple-element.23) | copy-start | bytes 196612
  76.5 0.9 %copy-start.1 = (f32[32,512]{1,0:T(8,128)S(1)}, f32[32,512]{1,0:T(8,128)}, u32[]{:S(2)}) copy-start(f32[32,512]{1,0:T(8,128)} %get-tuple-element.14) | copy-start | bytes 196612

commit v3 on v2

--- a/solution.py
+++ b/solution.py
@@ -111,7 +111,7 @@
     mix_own, mix_part, mix_send, mix_fwd, mix_recv,
     in_own, in_part, in_send, in_fwd, in_recv,
     g_own, g_send, g_recv, h_own, h_send, h_recv,
-    load_sem, send_sem, recv_sem,
+    load_sem, send_sem, recv_sem, ready_sem,
 ):
     seq, ch = lax.axis_index("seq"), lax.axis_index("ch")
     core, y, z = lax.rem(seq, 2), lax.rem(seq // 2, 4), seq // 8
@@ -136,10 +136,6 @@
             device_id=device,
             device_id_type=MESH,
         )
-
-    barrier = pltpu.get_barrier_semaphore()
-    for device in [x_peer(1), x_peer(3), core_peer] + [zy_peer(dz, dy) for dz, dy in shifts]:
-        pl.semaphore_signal(barrier, inc=1, device_id=device, device_id_type=MESH)
 
     loads = [
         pltpu.make_async_copy(src, dst, load_sem.at[n])
@@ -155,6 +151,11 @@
     ]
     for load in loads:
         load.start()
+
+    barrier = pltpu.get_barrier_semaphore()
+    y_peers = [zy_peer(0, k) for k in range(1, 4)]
+    for device in [x_peer(1), x_peer(3), core_peer] + y_peers + [zy_peer(k, 0) for k in range(1, 4)]:
+        pl.semaphore_signal(barrier, inc=1, device_id=device, device_id_type=MESH)
     anti = anti_identity()
     e = spread_matrix()
     small[...] = jnp.zeros_like(small)
@@ -164,8 +165,16 @@
         for k in range(BLOCKS):
             here, there = slice(k * Q, (k + 1) * Q), slice(D - (k + 1) * Q, D - k * Q)
             small[SMALL[1][at] : SMALL[1][at] + n, here] = mm(weight[:, there], anti).astype(BF16)
-    loads[0].wait()
-    pl.semaphore_wait(barrier, 2 + 1 + PEERS - 1)
+    for load in loads[:4]:
+        load.wait()
+    for k in range(BLOCKS):
+        here, there = slice(k * Q, (k + 1) * Q), slice(D - (k + 1) * Q, D - k * Q)
+        px_flip[here, :] = mm(anti, proj_x[there, :]).astype(BF16)
+        pz_flip[here, :] = mm(anti, proj_z[there, :]).astype(BF16)
+        hidden_flip[:, here] = mm(hidden[:, there], anti).astype(BF16)
+    pl.semaphore_wait(barrier, 9)
+    for device in y_peers:
+        pl.semaphore_signal(ready_sem, inc=1, device_id=device, device_id_type=MESH)
 
     half = [slice(0, Q), slice(Q, L)]
     before, after = lax.rem(ch + 3, 4), lax.rem(ch + 1, 4)
@@ -179,15 +188,6 @@
 
     for n in range(4):
         cot_copy(n).start()
-
-    loads[1].wait()
-    loads[2].wait()
-    loads[3].wait()
-    for k in range(BLOCKS):
-        here, there = slice(k * Q, (k + 1) * Q), slice(D - (k + 1) * Q, D - k * Q)
-        px_flip[here, :] = mm(anti, proj_x[there, :]).astype(BF16)
-        pz_flip[here, :] = mm(anti, proj_z[there, :]).astype(BF16)
-        hidden_flip[:, here] = mm(hidden[:, there], anti).astype(BF16)
 
     def project_step(k, carry):
         rows = rows_of(k)
@@ -205,10 +205,6 @@
         return carry
 
     lax.fori_loop(0, CHUNKS, project_step, 0)
-
-    for n in range(2):
-        cot_copy(n).wait_recv()
-        cot_copy(4 + n).start()
 
     def state_step(i, carry):
         strand, k = i // CHUNKS, lax.rem(i, CHUNKS)
@@ -231,6 +227,10 @@
         return carry
 
     lax.fori_loop(0, 2 * CHUNKS, state_step, 0)
+
+    for n in range(2):
+        cot_copy(n).wait_recv()
+        cot_copy(4 + n).start()
 
     def times(strand):
         return list(range(CHUNKS)) if strand == 0 else list(range(CHUNKS))[::-1]
@@ -368,6 +368,7 @@
 
         @pl.when(i == 0)
         def _():
+            pl.semaphore_wait(ready_sem, 3)
             round_a.spread_out()
 
         return carry
@@ -474,10 +475,12 @@
         def columns(self, r):
             return pl.ds(pl.multiple_of(lax.rem(ch + r, 4) * Q, Q), Q)
 
-        def begin(self):
+        def far(self):
             for n in range(2):
                 self.send[1, half[n], :] = self.compute(half[n], self.columns(2)).astype(BF16)
                 self.copy(n).start()
+
+        def near(self):
             self.send[0, half[1], :] = self.compute(half[1], self.columns(1)).astype(BF16)
             self.copy(2).start()
             self.send[2, half[0], :] = self.compute(half[0], self.columns(3)).astype(BF16)
@@ -526,7 +529,46 @@
 
     mix_sum = ColumnSum(S_MIX, mix_block, mix_own, mix_part, mix_send, mix_fwd, mix_recv)
     in_sum = ColumnSum(S_IN, in_block, in_own, in_part, in_send, in_fwd, in_recv)
-    mix_sum.begin()
+    mix_sum.far()
+    mix_sum.near()
+
+    def g_core_copy(n):
+        return remote(g_send.at[n, :, other], g_recv.at[n], S_GCORE + n, core_peer)
+
+    def g_peer_copy(n, dz, dy):
+        to = lax.rem(z + dz, 4) * 4 + lax.rem(y + dy, 4)
+        at = 4 * dz + dy
+        return remote(
+            h_send.at[n, to], h_recv.at[n, at], S_GPEER + PEERS * n + at, zy_peer(dz, dy)
+        )
+
+    def weight_part(n, left, left_flip, right):
+        def step(b, carry):
+            value = t_mm(left(b), right[0]) + t_mm(left_flip(b), right[1])
+            g_own[n, pl.ds(pl.multiple_of(b * 4, 4), 4)] = value.reshape(4, 2, ROWS, W)
+            g_send[n, pl.ds(pl.multiple_of(b * 4, 4), 4)] = value.astype(BF16).reshape(
+                4, 2, ROWS, W
+            )
+            return carry
+
+        lax.fori_loop(0, BLOCKS, step, 0)
+        g_core_copy(n).start()
+
+    def weight_pair(n):
+        g_core_copy(n).wait_recv()
+
+        def pair_sum(i, carry):
+            value = g_own[n, i, core] + g_recv[n, i].astype(F32)
+            h_send[n, i] = value.astype(BF16)
+            return carry
+
+        lax.fori_loop(0, PEERS, pair_sum, 0)
+        h_own[n] = g_own[n, place, core] + g_recv[n, place].astype(F32)
+        for dz, dy in shifts:
+            g_peer_copy(n, dz, dy).start()
+
+    weight_part(0, lambda b: cot[b], lambda b: cot_flip[b], os)
+    weight_part(1, lambda b: hidden[:, rows_of(b)], lambda b: hidden_flip[:, rows_of(b)], dzs)
 
     def inner_step(i, carry):
         strand, k = i // CHUNKS, lax.rem(i, CHUNKS)
@@ -560,57 +602,21 @@
         dbs[strand, rows, :] = mm(pairs, c)
         dcs[strand, rows, :] += t_mm(pairs, b)
 
+        @pl.when(i == 0)
+        def _():
+            mix_sum.middle()
+            weight_pair(0)
+
         @pl.when(i == 1)
         def _():
-            mix_sum.middle()
-
-        @pl.when(i == 2)
-        def _():
             round_b.collect()
 
         return carry
 
     lax.fori_loop(0, 2 * CHUNKS, inner_step, 0)
 
-    def g_core_copy(n):
-        return remote(g_send.at[n, :, other], g_recv.at[n], S_GCORE + n, core_peer)
-
-    def g_peer_copy(n, dz, dy):
-        to = lax.rem(z + dz, 4) * 4 + lax.rem(y + dy, 4)
-        at = 4 * dz + dy
-        return remote(
-            h_send.at[n, to], h_recv.at[n, at], S_GPEER + PEERS * n + at, zy_peer(dz, dy)
-        )
-
-    def weight_part(n, left, left_flip, right):
-        def step(b, carry):
-            value = t_mm(left(b), right[0]) + t_mm(left_flip(b), right[1])
-            g_own[n, pl.ds(pl.multiple_of(b * 4, 4), 4)] = value.reshape(4, 2, ROWS, W)
-            g_send[n, pl.ds(pl.multiple_of(b * 4, 4), 4)] = value.astype(BF16).reshape(
-                4, 2, ROWS, W
-            )
-            return carry
-
-        lax.fori_loop(0, BLOCKS, step, 0)
-        g_core_copy(n).start()
-
-    def weight_pair(n):
-        g_core_copy(n).wait_recv()
-
-        def pair_sum(i, carry):
-            value = g_own[n, i, core] + g_recv[n, i].astype(F32)
-            h_send[n, i] = value.astype(BF16)
-            return carry
-
-        lax.fori_loop(0, PEERS, pair_sum, 0)
-        h_own[n] = g_own[n, place, core] + g_recv[n, place].astype(F32)
-        for dz, dy in shifts:
-            g_peer_copy(n, dz, dy).start()
-
-    weight_part(0, lambda b: cot[b], lambda b: cot_flip[b], os)
-    weight_part(1, lambda b: hidden[:, rows_of(b)], lambda b: hidden_flip[:, rows_of(b)], dzs)
     mix_sum.own_block()
-    weight_pair(0)
+    weight_pair(1)
 
     up, down = round_b.take()
     for strand, grad in enumerate((down, up)):
@@ -648,9 +654,9 @@
 
     lax.fori_loop(0, CHUNKS, back_step, 0)
 
+    in_sum.far()
     weight_part(2, lambda b: hidden[:, rows_of(b)], lambda b: hidden_flip[:, rows_of(b)], dxs)
-    in_sum.begin()
-    weight_pair(1)
+    in_sum.near()
     weight_pair(2)
     in_sum.middle()
     in_sum.own_block()
@@ -692,6 +698,15 @@
             g_peer_copy(n, dz, dy).wait_send()
 
 
+def hand_over(*refs):
+    sems = refs[10]
+    copies = [pltpu.make_async_copy(refs[n], refs[5 + n], sems.at[n]) for n in range(5)]
+    for copy in copies:
+        copy.start()
+    for copy in copies:
+        copy.wait()
+
+
 def shape(*dims, dtype=F32):
     return jax.ShapeDtypeStruct(dims, dtype)
 
@@ -704,15 +719,16 @@
 ):
     bias, rate, skip = (v[None, :] for v in (dt_bias, decay_rate, skip_gain))
     vm = pltpu.VMEM
-    block_out, grad_hidden, grad_x, grad_z, grad_out = pl.pallas_call(
+    results = (
+        shape(L, Q, dtype=BF16),
+        shape(L, Q),
+        shape(ROWS, W),
+        shape(ROWS, W),
+        shape(ROWS, W),
+    )
+    made = pl.pallas_call(
         block_kernel,
-        out_shape=(
-            shape(L, Q, dtype=BF16),
-            shape(L, Q),
-            shape(ROWS, W),
-            shape(ROWS, W),
-            shape(ROWS, W),
-        ),
+        out_shape=results,
         in_specs=[pl.BlockSpec(memory_space=pl.ANY)] * 5 + [VMEM] * 6,
         out_specs=[VMEM] * 5,
         scratch_shapes=[
@@ -742,6 +758,7 @@
             vm((3, PEERS, ROWS, W), BF16),
             pltpu.SemaphoreType.DMA((5,)),
             pltpu.SemaphoreType.DMA((S_ALL,)), pltpu.SemaphoreType.DMA((S_ALL,)),
+            pltpu.SemaphoreType.REGULAR,
         ],
         compiler_params=pltpu.CompilerParams(
             vmem_limit_bytes=60 * 2**20, collective_id=0, has_side_effects=True
@@ -751,7 +768,15 @@
         hidden, proj_x, proj_z, proj_out, cotangent,
         proj_b.T, proj_c.T, proj_dt.T, bias, rate, skip,
     )
-    return block_out, grad_hidden, grad_x, grad_z, grad_out.T
+    *most, grad_out = pl.pallas_call(
+        hand_over,
+        out_shape=results,
+        in_specs=[pl.BlockSpec(memory_space=pl.ANY)] * 5,
+        out_specs=[pl.BlockSpec(memory_space=pl.ANY)] * 5,
+        scratch_shapes=[pltpu.SemaphoreType.DMA((5,))],
+        name="hand_over",
+    )(*made)
+    return *most, grad_out.T
 
 
 def solution(mesh):

time: 79.1 us -> 94.8 us (1.20)
  Pallas kernels: 72.4 us -> 93.7 us
  local copies, waits for them, and re-layouts: 4.95 us -> 0 us
    pallas_call x1 -> x2, Pallas kernels: 72.4 us -> 93.7 us  [the longest x1 62.8 us: body(): pl.pallas_call(block_kernel, out_shape=results, in_specs=[pl.BlockSpec(me...]
    unnamed x13 -> x0, local copies, waits for them, and re-layouts: 4.95 us -> none
where the time goes in v3:
time: 94.8 us; the launch traced here: 94.3 us
  Pallas kernels  93.7 us (99%)
    pallas_call x1, Pallas kernels, body(): pl.pallas_call(block_kernel, out_shape=results, in_specs=[pl.BlockSpec(me...  62.8 us
    pallas_call x1, Pallas kernels, body(): pl.pallas_call(hand_over, out_shape=results, in_specs=[pl.BlockSpec(memor...  30.9 us

profile of v3, /device:TPU:1, one launch (start us, length us, event | category | flops | bytes accessed | tf_op | source)
XLA Modules:
  0.0 94.3 jit_solution(18240864282859702576)
XLA Ops:
  0.6 62.8 %block.1 = (bf16[512,256]{1,0:T(8,128)(2,1)}, f32[512,256]{1,0:T(8,128)}, f32[32,512]{1,0:T(8,128)}, f32[32,512]{1,0:T(8,128)}, f32[32,512]{1,0:T(8,128)}) custom-call(bf16[512,1024]{1,0:T(8,128)(2,1)} %hidden_hbm.1, bf16[1024,512]{1,0:T(8,128)(2,1)} %proj_x_hbm.1, bf16[1024,512]{1,0:T(8,128)(2,1)} %proj_z_hbm.1, bf16[512,1024]{1,0:T(8,128)(2,1)} %proj_out_hbm.1, ...), custom_call_target="tpu_custom_call" | custom-call | tf_op jit(solution)/shard_map/block/pallas_call | solution.py:729
  63.4 30.9 %hand_over.1 = (bf16[512,256]{1,0:T(8,128)(2,1)}, f32[512,256]{1,0:T(8,128)}, f32[32,512]{1,0:T(8,128)}, f32[32,512]{1,0:T(8,128)}, f32[32,512]{1,0:T(8,128)}) custom-call(bf16[512,256]{1,0:T(8,128)(2,1)} %get-tuple-element.15.refs_0_, f32[512,256]{1,0:T(8,128)} %get-tuple-element.16.refs_1_, f32[32,512]{1,0:T(8,128)} %get-tuple-element.17.refs_2_, ...), custom_call_target="tpu_custom_call" | custom-call | tf_op jit(solution)/shard_map/hand_over/pallas_call | solution.py:771

commit v4 on v3

--- a/solution.py
+++ b/solution.py
@@ -58,22 +58,27 @@
     return lax.broadcasted_iota(jnp.int32, shape, dim)
 
 
+def identity():
+    return jnp.where(iota((Q, Q), 0) == iota((Q, Q), 1), 1.0, 0.0).astype(BF16)
+
+
 def anti_identity():
     return jnp.where(iota((Q, Q), 0) + iota((Q, Q), 1) == Q - 1, 1.0, 0.0).astype(BF16)
 
 
 def spread_matrix():
-    return jnp.where(iota((HEADS, W), 1) // HEAD == iota((HEADS, W), 0), 1.0, 0.0).astype(BF16)
+    head = iota((2 * HEADS, W), 0)
+    head = jnp.where(head >= HEADS, head - HEADS, head)
+    return jnp.where(iota((2 * HEADS, W), 1) // HEAD == head, 1.0, 0.0).astype(BF16)
 
 
 def spread(v, e):
-    high, low = split2(v)
-    return mm(high, e) + mm(low, e)
+    return mm(jnp.concatenate(split2(v), axis=1), e)
 
 
 def gather_heads(v, e):
     high, low = split2(v)
-    return mm_t(high, e) + mm_t(low, e)
+    return (mm_t(high, e) + mm_t(low, e))[:, 0:HEADS]
 
 
 def order(sign):
@@ -102,7 +107,7 @@
     proj_b, proj_c, proj_dt, bias, rate, skip,
     block_out, grad_hidden, grad_x, grad_z, grad_out,
     hidden, proj_x, proj_z, proj_out,
-    px_flip, pz_flip, po_flip, small, hidden_flip, cot, cot_flip,
+    px_flip, pz_flip, po_flip, small, hidden_t, hidden_flip_t, cot, cot_t, cot_flip_t,
     xs, zs, bs, cs, dts, dos, cums, dts_soft, e_cums, e_rests, dt_wides, dyb, xdt, zacc,
     yi, gi, dcs, dbs, dyy, ext, os, dxs, dzs,
     chunk_state, chunk_grad, chunk_decay, chunk_dot,
@@ -165,13 +170,7 @@
         for k in range(BLOCKS):
             here, there = slice(k * Q, (k + 1) * Q), slice(D - (k + 1) * Q, D - k * Q)
             small[SMALL[1][at] : SMALL[1][at] + n, here] = mm(weight[:, there], anti).astype(BF16)
-    for load in loads[:4]:
-        load.wait()
-    for k in range(BLOCKS):
-        here, there = slice(k * Q, (k + 1) * Q), slice(D - (k + 1) * Q, D - k * Q)
-        px_flip[here, :] = mm(anti, proj_x[there, :]).astype(BF16)
-        pz_flip[here, :] = mm(anti, proj_z[there, :]).astype(BF16)
-        hidden_flip[:, here] = mm(hidden[:, there], anti).astype(BF16)
+    loads[0].wait()
     pl.semaphore_wait(barrier, 9)
     for device in y_peers:
         pl.semaphore_signal(ready_sem, inc=1, device_id=device, device_id_type=MESH)
@@ -188,6 +187,18 @@
 
     for n in range(4):
         cot_copy(n).start()
+
+    loads[1].wait()
+    ident = identity()
+    for k in range(BLOCKS):
+        here, there = slice(k * Q, (k + 1) * Q), slice(D - (k + 1) * Q, D - k * Q)
+        hidden_t[k] = mm_t(ident, hidden[:, here]).astype(BF16)
+        hidden_flip_t[k] = mm_t(anti, hidden[:, there]).astype(BF16)
+    for load, source, flip in ((loads[2], proj_x, px_flip), (loads[3], proj_z, pz_flip)):
+        load.wait()
+        for k in range(BLOCKS):
+            here, there = slice(k * Q, (k + 1) * Q), slice(D - (k + 1) * Q, D - k * Q)
+            flip[here, :] = mm(anti, source[there, :]).astype(BF16)
 
     def project_step(k, carry):
         rows = rows_of(k)
@@ -388,7 +399,8 @@
         rows = rows_of(k)
         forward = backward = None
         for b in range(BLOCKS):
-            cot_flip[b, rows, :] = mm(cot[BLOCKS - 1 - b, rows, :], anti).astype(BF16)
+            cot_t[b, :, rows] = mm_t(ident, cot[b, rows, :]).astype(BF16)
+            cot_flip_t[b, :, rows] = mm_t(anti, cot[BLOCKS - 1 - b, rows, :]).astype(BF16)
             columns = slice(b * Q, (b + 1) * Q)
             part = mm_t(cot[b, rows, :], proj_out[:, columns])
             part_flip = mm_t(cot[b, rows, :], po_flip[:, columns])
@@ -533,7 +545,7 @@
     mix_sum.near()
 
     def g_core_copy(n):
-        return remote(g_send.at[n, :, other], g_recv.at[n], S_GCORE + n, core_peer)
+        return remote(g_send.at[n], g_recv.at[n], S_GCORE + n, core_peer)
 
     def g_peer_copy(n, dz, dy):
         to = lax.rem(z + dz, 4) * 4 + lax.rem(y + dy, 4)
@@ -544,11 +556,11 @@
 
     def weight_part(n, left, left_flip, right):
         def step(b, carry):
-            value = t_mm(left(b), right[0]) + t_mm(left_flip(b), right[1])
-            g_own[n, pl.ds(pl.multiple_of(b * 4, 4), 4)] = value.reshape(4, 2, ROWS, W)
-            g_send[n, pl.ds(pl.multiple_of(b * 4, 4), 4)] = value.astype(BF16).reshape(
-                4, 2, ROWS, W
-            )
+            value = mm(left[b], right[0]) + mm(left_flip[b], right[1])
+            value = value.reshape(4, 2, ROWS, W)
+            at = pl.ds(pl.multiple_of(b * 4, 4), 4)
+            g_own[n, at] = jnp.where(core == 0, value[:, 0], value[:, 1])
+            g_send[n, at] = jnp.where(core == 0, value[:, 1], value[:, 0]).astype(BF16)
             return carry
 
         lax.fori_loop(0, BLOCKS, step, 0)
@@ -558,17 +570,17 @@
         g_core_copy(n).wait_recv()
 
         def pair_sum(i, carry):
-            value = g_own[n, i, core] + g_recv[n, i].astype(F32)
+            value = g_own[n, i] + g_recv[n, i].astype(F32)
             h_send[n, i] = value.astype(BF16)
             return carry
 
         lax.fori_loop(0, PEERS, pair_sum, 0)
-        h_own[n] = g_own[n, place, core] + g_recv[n, place].astype(F32)
+        h_own[n] = g_own[n, place] + g_recv[n, place].astype(F32)
         for dz, dy in shifts:
             g_peer_copy(n, dz, dy).start()
 
-    weight_part(0, lambda b: cot[b], lambda b: cot_flip[b], os)
-    weight_part(1, lambda b: hidden[:, rows_of(b)], lambda b: hidden_flip[:, rows_of(b)], dzs)
+    weight_part(0, cot_t, cot_flip_t, os)
+    weight_part(1, hidden_t, hidden_flip_t, dzs)
 
     def inner_step(i, carry):
         strand, k = i // CHUNKS, lax.rem(i, CHUNKS)
@@ -654,10 +666,10 @@
 
     lax.fori_loop(0, CHUNKS, back_step, 0)
 
+    weight_part(2, hidden_t, hidden_flip_t, dxs)
     in_sum.far()
-    weight_part(2, lambda b: hidden[:, rows_of(b)], lambda b: hidden_flip[:, rows_of(b)], dxs)
+    weight_pair(2)
     in_sum.near()
-    weight_pair(2)
     in_sum.middle()
     in_sum.own_block()
 
@@ -670,21 +682,26 @@
         return carry
 
     lax.fori_loop(0, CHUNKS, mix_step, 0)
-    in_sum.arrived()
-
-    def in_step(k, carry):
-        rows = rows_of(k)
-        grad_hidden[rows, :] = cot[ch, rows, :].astype(F32) + in_sum.finish(rows)
-        return carry
-
-    lax.fori_loop(0, CHUNKS, in_step, 0)
-
-    for n, out in enumerate((grad_out, grad_z, grad_x)):
+
+    def weight_total(n, out):
         total = h_own[n]
         for dz, dy in shifts:
             g_peer_copy(n, dz, dy).wait_recv()
             total = total + h_recv[n, 4 * dz + dy].astype(F32)
         out[...] = total
+
+    weight_total(0, grad_out)
+    weight_total(1, grad_z)
+    in_sum.arrived()
+
+    def in_step(k, carry):
+        rows = rows_of(k)
+        grad_hidden[rows, :] = cot[ch, rows, :].astype(F32) + in_sum.finish(rows)
+        return carry
+
+    lax.fori_loop(0, CHUNKS, in_step, 0)
+
+    weight_total(2, grad_x)
 
     for n in range(6):
         cot_copy(n).wait_send()
@@ -734,7 +751,8 @@
         scratch_shapes=[
             vm((L, D), BF16), vm((D, W), BF16), vm((D, W), BF16), vm((W, D), BF16),
             vm((D, W), BF16), vm((D, W), BF16), vm((W, D), BF16), vm((128, D), BF16),
-            vm((L, D), BF16), vm((BLOCKS, L, Q), BF16), vm((BLOCKS, L, Q), BF16),
+            vm((BLOCKS, Q, L), BF16), vm((BLOCKS, Q, L), BF16),
+            vm((BLOCKS, L, Q), BF16), vm((BLOCKS, Q, L), BF16), vm((BLOCKS, Q, L), BF16),
             vm((2, L, W), F32), vm((2, L, W), F32), vm((2, L, NS), BF16), vm((2, L, NS), BF16),
             vm((2, L, HEADS), F32), vm((2, L, W), BF16), vm((2, L, HEADS), F32),
             vm((2, L, HEADS), F32), vm((2, L, W), F32), vm((2, L, W), F32), vm((2, L, W), F32),
@@ -752,7 +770,7 @@
             vm((2, L, Q), BF16),
             vm((L, Q), F32), vm((2, Q, Q), F32), vm((3, L, Q), BF16), vm((2, Q, Q), BF16),
             vm((2, L, Q), BF16),
-            vm((3, PEERS, 2, ROWS, W), F32), vm((3, PEERS, 2, ROWS, W), BF16),
+            vm((3, PEERS, ROWS, W), F32), vm((3, PEERS, ROWS, W), BF16),
             vm((3, PEERS, ROWS, W), BF16),
             vm((3, ROWS, W), F32), vm((3, PEERS, ROWS, W), BF16),
             vm((3, PEERS, ROWS, W), BF16),
@@ -771,7 +789,7 @@
     *most, grad_out = pl.pallas_call(
         hand_over,
         out_shape=results,
-        in_specs=[pl.BlockSpec(memory_space=pl.ANY)] * 5,
+        in_specs=[VMEM] * 5,
         out_specs=[pl.BlockSpec(memory_space=pl.ANY)] * 5,
         scratch_shapes=[pltpu.SemaphoreType.DMA((5,))],
         name="hand_over",

time: 94.8 us -> 66.8 us (0.70)
  Pallas kernels: 93.7 us -> 65.8 us
    pallas_call x1, Pallas kernels: 30.9 us -> 2.11 us  [body(): pl.pallas_call(hand_over, out_shape=results, in_specs=[VMEM] * 5, out_spe...]
where the time goes in v4:
time: 66.8 us; the launch traced here: 66.6 us
  Pallas kernels  65.8 us (99%)
  between operations  0.8 us (1%)
    pallas_call x1, Pallas kernels, body(): pl.pallas_call(block_kernel, out_shape=results, in_specs=[pl.BlockSpec(me...  63.7 us
    pallas_call x1, Pallas kernels, body(): pl.pallas_call(hand_over, out_shape=results, in_specs=[VMEM] * 5, out_spe...  2.11 us

profile of v4, /device:TPU:1, one launch (start us, length us, event | category | flops | bytes accessed | tf_op | source)
XLA Modules:
  0.0 66.6 jit_solution(10094205911723935160)
XLA Ops:
  0.6 63.7 %block.1 = (bf16[512,256]{1,0:T(8,128)(2,1)}, f32[512,256]{1,0:T(8,128)}, f32[32,512]{1,0:T(8,128)}, f32[32,512]{1,0:T(8,128)}, f32[32,512]{1,0:T(8,128)}) custom-call(bf16[512,1024]{1,0:T(8,128)(2,1)} %hidden_hbm.1, bf16[1024,512]{1,0:T(8,128)(2,1)} %proj_x_hbm.1, bf16[1024,512]{1,0:T(8,128)(2,1)} %proj_z_hbm.1, bf16[512,1024]{1,0:T(8,128)(2,1)} %proj_out_hbm.1, ...), custom_call_target="tpu_custom_call" | custom-call | tf_op jit(solution)/shard_map/block/pallas_call | solution.py:746
  64.3 2.1 %hand_over.1 = (bf16[512,256]{1,0:T(8,128)(2,1)}, f32[512,256]{1,0:T(8,128)}, f32[32,512]{1,0:T(8,128)}, f32[32,512]{1,0:T(8,128)}, f32[32,512]{1,0:T(8,128)}) custom-call(bf16[512,256]{1,0:T(8,128)(2,1)} %get-tuple-element.15.refs_0_, f32[512,256]{1,0:T(8,128)} %get-tuple-element.16.refs_1_, f32[32,512]{1,0:T(8,128)} %get-tuple-element.17.refs_2_, ...), custom_call_target="tpu_custom_call" | custom-call | tf_op jit(solution)/shard_map/hand_over/pallas_call | solution.py:789

commit v5 on v4

--- a/solution.py
+++ b/solution.py
@@ -27,7 +27,7 @@
 
 S_COT, S_MIX, S_IN, S_A, S_B = 0, 6, 12, 18, 36
 S_GCORE, S_GPEER = 54, 57
-S_ALL = S_GPEER + 3 * 16
+S_ALL = S_GPEER + 3 * 12
 
 
 def mm(a, b):
@@ -115,7 +115,7 @@
     b_msg, b_core, b_pair, b_slots, b_back, b_in,
     mix_own, mix_part, mix_send, mix_fwd, mix_recv,
     in_own, in_part, in_send, in_fwd, in_recv,
-    g_own, g_send, g_recv, h_own, h_send, h_recv,
+    g_own, g_send, g_recv, h_send, h_recv, t_send, t_recv, t_own,
     load_sem, send_sem, recv_sem, ready_sem,
 ):
     seq, ch = lax.axis_index("seq"), lax.axis_index("ch")
@@ -154,13 +154,12 @@
             )
         )
     ]
-    for load in loads:
-        load.start()
-
     barrier = pltpu.get_barrier_semaphore()
     y_peers = [zy_peer(0, k) for k in range(1, 4)]
     for device in [x_peer(1), x_peer(3), core_peer] + y_peers + [zy_peer(k, 0) for k in range(1, 4)]:
         pl.semaphore_signal(barrier, inc=1, device_id=device, device_id_type=MESH)
+    for load in loads:
+        load.start()
     anti = anti_identity()
     e = spread_matrix()
     small[...] = jnp.zeros_like(small)
@@ -172,9 +171,6 @@
             small[SMALL[1][at] : SMALL[1][at] + n, here] = mm(weight[:, there], anti).astype(BF16)
     loads[0].wait()
     pl.semaphore_wait(barrier, 9)
-    for device in y_peers:
-        pl.semaphore_signal(ready_sem, inc=1, device_id=device, device_id_type=MESH)
-
     half = [slice(0, Q), slice(Q, L)]
     before, after = lax.rem(ch + 3, 4), lax.rem(ch + 1, 4)
 
@@ -187,6 +183,8 @@
 
     for n in range(4):
         cot_copy(n).start()
+    for device in y_peers:
+        pl.semaphore_signal(ready_sem, inc=1, device_id=device, device_id_type=MESH)
 
     loads[1].wait()
     ident = identity()
@@ -390,7 +388,6 @@
     for k in range(BLOCKS):
         here, there = slice(k * Q, (k + 1) * Q), slice(D - (k + 1) * Q, D - k * Q)
         po_flip[:, here] = mm(proj_out[:, there], anti).astype(BF16)
-    round_a.collect()
 
     for n in range(2, 6):
         cot_copy(n).wait_recv()
@@ -433,6 +430,7 @@
         two_halves(b_msg, slice(16 - 16 * strand, 32 - 16 * strand), grad)
     round_b.to_core().start()
 
+    round_a.collect()
     for strand, state in enumerate(round_a.take()):
         for k in times(strand):
             own_state = chunk_state[strand, k]
@@ -541,26 +539,27 @@
 
     mix_sum = ColumnSum(S_MIX, mix_block, mix_own, mix_part, mix_send, mix_fwd, mix_recv)
     in_sum = ColumnSum(S_IN, in_block, in_own, in_part, in_send, in_fwd, in_recv)
-    mix_sum.far()
-    mix_sum.near()
 
     def g_core_copy(n):
         return remote(g_send.at[n], g_recv.at[n], S_GCORE + n, core_peer)
 
-    def g_peer_copy(n, dz, dy):
-        to = lax.rem(z + dz, 4) * 4 + lax.rem(y + dy, 4)
-        at = 4 * dz + dy
-        return remote(
-            h_send.at[n, to], h_recv.at[n, at], S_GPEER + PEERS * n + at, zy_peer(dz, dy)
-        )
+    def g_copy(n, at):
+        stage, over_z, k = at // 6, at % 6 // 3, at % 3 + 1
+        peer = zy_peer(k, 0) if over_z != stage else zy_peer(0, k)
+        if stage:
+            src, dst = t_send.at[n, over_z, k - 1], t_recv.at[n, over_z, k - 1]
+        elif over_z:
+            src, dst = h_send.at[n, lax.rem(z + k, 4), :, :, Q:W], h_recv.at[n, 1, k - 1]
+        else:
+            src, dst = h_send.at[n, :, lax.rem(y + k, 4), :, 0:Q], h_recv.at[n, 0, k - 1]
+        return remote(src, dst, S_GPEER + 12 * n + at, peer)
 
     def weight_part(n, left, left_flip, right):
         def step(b, carry):
             value = mm(left[b], right[0]) + mm(left_flip[b], right[1])
             value = value.reshape(4, 2, ROWS, W)
-            at = pl.ds(pl.multiple_of(b * 4, 4), 4)
-            g_own[n, at] = jnp.where(core == 0, value[:, 0], value[:, 1])
-            g_send[n, at] = jnp.where(core == 0, value[:, 1], value[:, 0]).astype(BF16)
+            g_own[n, b] = jnp.where(core == 0, value[:, 0], value[:, 1])
+            g_send[n, b] = jnp.where(core == 0, value[:, 1], value[:, 0]).astype(BF16)
             return carry
 
         lax.fori_loop(0, BLOCKS, step, 0)
@@ -570,17 +569,48 @@
         g_core_copy(n).wait_recv()
 
         def pair_sum(i, carry):
-            value = g_own[n, i] + g_recv[n, i].astype(F32)
-            h_send[n, i] = value.astype(BF16)
+            at = (n, i // 4, lax.rem(i, 4))
+            value = g_own[at] + g_recv[at].astype(F32)
+            g_own[at] = value
+            h_send[at] = value.astype(BF16)
             return carry
 
         lax.fori_loop(0, PEERS, pair_sum, 0)
-        h_own[n] = g_own[n, place] + g_recv[n, place].astype(F32)
-        for dz, dy in shifts:
-            g_peer_copy(n, dz, dy).start()
+        for at in range(6):
+            g_copy(n, at).start()
+
+    def weight_middle(n):
+        for at in range(6):
+            g_copy(n, at).wait_recv()
+        for r in (1, 2, 3, 0):
+            to_z, to_y = lax.rem(z + r, 4), lax.rem(y + r, 4)
+            first, second = g_own[n, to_z, y, :, 0:Q], g_own[n, z, to_y, :, Q:W]
+            for k in range(3):
+                first = first + h_recv[n, 0, k, to_z].astype(F32)
+                second = second + h_recv[n, 1, k, to_y].astype(F32)
+            if r:
+                t_send[n, 0, r - 1] = first.astype(BF16)
+                t_send[n, 1, r - 1] = second.astype(BF16)
+                g_copy(n, 6 + r - 1).start()
+                g_copy(n, 9 + r - 1).start()
+            else:
+                t_own[n, 0] = first
+                t_own[n, 1] = second
+
+    def weight_total(n, out):
+        for at in range(6, 12):
+            g_copy(n, at).wait_recv()
+        for side in range(2):
+            total = t_own[n, side]
+            for k in range(3):
+                total = total + t_recv[n, side, k].astype(F32)
+            out[:, side * Q : (side + 1) * Q] = total
 
     weight_part(0, cot_t, cot_flip_t, os)
+    mix_sum.far()
+    mix_sum.near()
     weight_part(1, hidden_t, hidden_flip_t, dzs)
+    weight_pair(0)
 
     def inner_step(i, carry):
         strand, k = i // CHUNKS, lax.rem(i, CHUNKS)
@@ -617,18 +647,22 @@
         @pl.when(i == 0)
         def _():
             mix_sum.middle()
-            weight_pair(0)
+            weight_pair(1)
 
         @pl.when(i == 1)
         def _():
             round_b.collect()
 
+        @pl.when(i == 2)
+        def _():
+            weight_middle(0)
+
         return carry
 
     lax.fori_loop(0, 2 * CHUNKS, inner_step, 0)
 
     mix_sum.own_block()
-    weight_pair(1)
+    weight_middle(1)
 
     up, down = round_b.take()
     for strand, grad in enumerate((down, up)):
@@ -672,6 +706,7 @@
     in_sum.near()
     in_sum.middle()
     in_sum.own_block()
+    weight_middle(2)
 
     mix_sum.arrived()
 
@@ -682,13 +717,6 @@
         return carry
 
     lax.fori_loop(0, CHUNKS, mix_step, 0)
-
-    def weight_total(n, out):
-        total = h_own[n]
-        for dz, dy in shifts:
-            g_peer_copy(n, dz, dy).wait_recv()
-            total = total + h_recv[n, 4 * dz + dy].astype(F32)
-        out[...] = total
 
     weight_total(0, grad_out)
     weight_total(1, grad_z)
@@ -711,8 +739,8 @@
     in_sum.drain()
     for n in range(3):
         g_core_copy(n).wait_send()
-        for dz, dy in shifts:
-            g_peer_copy(n, dz, dy).wait_send()
+        for at in range(12):
+            g_copy(n, at).wait_send()
 
 
 def hand_over(*refs):
@@ -770,10 +798,10 @@
             vm((2, L, Q), BF16),
             vm((L, Q), F32), vm((2, Q, Q), F32), vm((3, L, Q), BF16), vm((2, Q, Q), BF16),
             vm((2, L, Q), BF16),
-            vm((3, PEERS, ROWS, W), F32), vm((3, PEERS, ROWS, W), BF16),
-            vm((3, PEERS, ROWS, W), BF16),
-            vm((3, ROWS, W), F32), vm((3, PEERS, ROWS, W), BF16),
-            vm((3, PEERS, ROWS, W), BF16),
+            vm((3, 4, 4, ROWS, W), F32), vm((3, 4, 4, ROWS, W), BF16),
+            vm((3, 4, 4, ROWS, W), BF16), vm((3, 4, 4, ROWS, W), BF16),
+            vm((3, 2, 3, 4, ROWS, Q), BF16), vm((3, 2, 3, ROWS, Q), BF16),
+            vm((3, 2, 3, ROWS, Q), BF16), vm((3, 2, ROWS, Q), F32),
             pltpu.SemaphoreType.DMA((5,)),
             pltpu.SemaphoreType.DMA((S_ALL,)), pltpu.SemaphoreType.DMA((S_ALL,)),
             pltpu.SemaphoreType.REGULAR,

time: 66.8 us -> 67.5 us (1.010)
  Pallas kernels: 65.8 us -> 66.5 us
    pallas_call x1, Pallas kernels: 63.7 us -> 64.4 us  [body(): pl.pallas_call(block_kernel, out_shape=results, in_specs=[pl.BlockSpec(me...]
where the time goes in v5:
time: 67.5 us; the launch traced here: 67.3 us
  Pallas kernels  66.5 us (99%)
  between operations  0.8 us (1%)
    pallas_call x1, Pallas kernels, body(): pl.pallas_call(block_kernel, out_shape=results, in_specs=[pl.BlockSpec(me...  64.4 us
    pallas_call x1, Pallas kernels, body(): pl.pallas_call(hand_over, out_shape=results, in_specs=[VMEM] * 5, out_spe...  2.11 us

profile of v5, /device:TPU:1, one launch (start us, length us, event | category | flops | bytes accessed | tf_op | source)
XLA Modules:
  0.0 67.3 jit_solution(7196847933151966828)
XLA Ops:
  0.6 64.4 %block.1 = (bf16[512,256]{1,0:T(8,128)(2,1)}, f32[512,256]{1,0:T(8,128)}, f32[32,512]{1,0:T(8,128)}, f32[32,512]{1,0:T(8,128)}, f32[32,512]{1,0:T(8,128)}) custom-call(bf16[512,1024]{1,0:T(8,128)(2,1)} %hidden_hbm.1, bf16[1024,512]{1,0:T(8,128)(2,1)} %proj_x_hbm.1, bf16[1024,512]{1,0:T(8,128)(2,1)} %proj_z_hbm.1, bf16[512,1024]{1,0:T(8,128)(2,1)} %proj_out_hbm.1, ...), custom_call_target="tpu_custom_call" | custom-call | tf_op jit(solution)/shard_map/block/pallas_call | solution.py:774
  65.1 2.1 %hand_over.1 = (bf16[512,256]{1,0:T(8,128)(2,1)}, f32[512,256]{1,0:T(8,128)}, f32[32,512]{1,0:T(8,128)}, f32[32,512]{1,0:T(8,128)}, f32[32,512]{1,0:T(8,128)}) custom-call(bf16[512,256]{1,0:T(8,128)(2,1)} %get-tuple-element.15.refs_0_, f32[512,256]{1,0:T(8,128)} %get-tuple-element.16.refs_1_, f32[32,512]{1,0:T(8,128)} %get-tuple-element.17.refs_2_, ...), custom_call_target="tpu_custom_call" | custom-call | tf_op jit(solution)/shard_map/hand_over/pallas_call | solution.py:817

commit v6 on v5

--- a/solution.py
+++ b/solution.py
@@ -27,7 +27,8 @@
 
 S_COT, S_MIX, S_IN, S_A, S_B = 0, 6, 12, 18, 36
 S_GCORE, S_GPEER = 54, 57
-S_ALL = S_GPEER + 3 * 12
+S_LAST = S_GPEER + 2 * 12
+S_ALL = S_LAST + 16
 
 
 def mm(a, b):
@@ -104,9 +105,9 @@
 
 def block_kernel(
     hidden_hbm, proj_x_hbm, proj_z_hbm, proj_out_hbm, cot_hbm,
-    proj_b, proj_c, proj_dt, bias, rate, skip,
+    proj_b_hbm, proj_c_hbm, proj_dt_hbm, bias_hbm, rate_hbm, skip_hbm,
     block_out, grad_hidden, grad_x, grad_z, grad_out,
-    hidden, proj_x, proj_z, proj_out,
+    hidden, proj_x, proj_z, proj_out, proj_b, proj_c, proj_dt, bias, rate, skip,
     px_flip, pz_flip, po_flip, small, hidden_t, hidden_flip_t, cot, cot_t, cot_flip_t,
     xs, zs, bs, cs, dts, dos, cums, dts_soft, e_cums, e_rests, dt_wides, dyb, xdt, zacc,
     yi, gi, dcs, dbs, dyy, ext, os, dxs, dzs,
@@ -115,7 +116,7 @@
     b_msg, b_core, b_pair, b_slots, b_back, b_in,
     mix_own, mix_part, mix_send, mix_fwd, mix_recv,
     in_own, in_part, in_send, in_fwd, in_recv,
-    g_own, g_send, g_recv, h_send, h_recv, t_send, t_recv, t_own,
+    g_own, g_send, g_recv, h_send, h_recv, t_send, t_recv, t_own, last_recv,
     load_sem, send_sem, recv_sem, ready_sem,
 ):
     seq, ch = lax.axis_index("seq"), lax.axis_index("ch")
@@ -151,17 +152,49 @@
                 (proj_x_hbm, proj_x),
                 (proj_z_hbm, proj_z),
                 (proj_out_hbm, proj_out),
+                (proj_b_hbm, proj_b),
+                (proj_c_hbm, proj_c),
+                (proj_dt_hbm, proj_dt),
+                (bias_hbm, bias),
+                (rate_hbm, rate),
+                (skip_hbm, skip),
             )
         )
     ]
     barrier = pltpu.get_barrier_semaphore()
-    y_peers = [zy_peer(0, k) for k in range(1, 4)]
-    for device in [x_peer(1), x_peer(3), core_peer] + y_peers + [zy_peer(k, 0) for k in range(1, 4)]:
+    near = [zy_peer(0, 1), zy_peer(0, 3), zy_peer(1, 0), zy_peer(3, 0)]
+    for device in [x_peer(1), x_peer(3), core_peer] + near:
         pl.semaphore_signal(barrier, inc=1, device_id=device, device_id_type=MESH)
-    for load in loads:
+    for load in loads[:1] + loads[5:] + loads[1:5]:
         load.start()
     anti = anti_identity()
     e = spread_matrix()
+    loads[0].wait()
+    pl.semaphore_wait(barrier, 7)
+    half = [slice(0, Q), slice(Q, L)]
+    before, after = lax.rem(ch + 3, 4), lax.rem(ch + 1, 4)
+
+    def cot_copy(n):
+        block, rows, to = (
+            (ch, half[0], 1), (ch, half[1], 3), (ch, half[1], 1), (ch, half[0], 3),
+            (before, half[0], 1), (after, half[1], 3),
+        )[n]
+        return remote(cot.at[block, rows], cot.at[block, rows], S_COT + n, x_peer(to))
+
+    for n in range(4):
+        cot_copy(n).start()
+    def vouch(n):
+        if n:
+            pl.semaphore_wait(ready_sem.at[n - 1], 4)
+        if n < 3:
+            for device in near:
+                pl.semaphore_signal(
+                    ready_sem.at[n], inc=1, device_id=device, device_id_type=MESH
+                )
+
+    vouch(0)
+    for load in loads[5:]:
+        load.wait()
     small[...] = jnp.zeros_like(small)
     for weight, at in zip((proj_b, proj_c, proj_dt), range(3)):
         n = weight.shape[0]
@@ -169,23 +202,6 @@
         for k in range(BLOCKS):
             here, there = slice(k * Q, (k + 1) * Q), slice(D - (k + 1) * Q, D - k * Q)
             small[SMALL[1][at] : SMALL[1][at] + n, here] = mm(weight[:, there], anti).astype(BF16)
-    loads[0].wait()
-    pl.semaphore_wait(barrier, 9)
-    half = [slice(0, Q), slice(Q, L)]
-    before, after = lax.rem(ch + 3, 4), lax.rem(ch + 1, 4)
-
-    def cot_copy(n):
-        block, rows, to = (
-            (ch, half[0], 1), (ch, half[1], 3), (ch, half[1], 1), (ch, half[0], 3),
-            (before, half[0], 1), (after, half[1], 3),
-        )[n]
-        return remote(cot.at[block, rows], cot.at[block, rows], S_COT + n, x_peer(to))
-
-    for n in range(4):
-        cot_copy(n).start()
-    for device in y_peers:
-        pl.semaphore_signal(ready_sem, inc=1, device_id=device, device_id_type=MESH)
-
     loads[1].wait()
     ident = identity()
     for k in range(BLOCKS):
@@ -214,6 +230,7 @@
         return carry
 
     lax.fori_loop(0, CHUNKS, project_step, 0)
+    vouch(1)
 
     def state_step(i, carry):
         strand, k = i // CHUNKS, lax.rem(i, CHUNKS)
@@ -236,6 +253,7 @@
         return carry
 
     lax.fori_loop(0, 2 * CHUNKS, state_step, 0)
+    vouch(2)
 
     for n in range(2):
         cot_copy(n).wait_recv()
@@ -377,7 +395,7 @@
 
         @pl.when(i == 0)
         def _():
-            pl.semaphore_wait(ready_sem, 3)
+            vouch(3)
             round_a.spread_out()
 
         return carry
@@ -389,25 +407,33 @@
         here, there = slice(k * Q, (k + 1) * Q), slice(D - (k + 1) * Q, D - k * Q)
         po_flip[:, here] = mm(proj_out[:, there], anti).astype(BF16)
 
-    for n in range(2, 6):
+    def cot_block(c, rows):
+        block = cot[c, rows, :]
+        cot_t[c, :, rows] = mm_t(ident, block).astype(BF16)
+        cot_flip_t[BLOCKS - 1 - c, :, rows] = mm_t(anti, block).astype(BF16)
+        columns = pl.ds(pl.multiple_of(c * Q, Q), Q)
+        return mm_t(block, proj_out[:, columns]), mm_t(block, po_flip[:, columns])
+
+    def first_step(k, carry):
+        rows = rows_of(k)
+        parts = [cot_block(c, rows) for c in (ch, before, after)]
+        for strand in range(2):
+            gi[strand, rows, :] = sum(part[strand] for part in parts)
+        return carry
+
+    def last_step(k, carry):
+        rows = rows_of(k)
+        parts = cot_block(lax.rem(ch + 2, 4), rows)
+        for strand in range(2):
+            dos[strand, rows, :] = (gi[strand, rows, :] + parts[strand]).astype(BF16)
+        return carry
+
+    for n in range(2, 4):
         cot_copy(n).wait_recv()
-
-    def cot_step(k, carry):
-        rows = rows_of(k)
-        forward = backward = None
-        for b in range(BLOCKS):
-            cot_t[b, :, rows] = mm_t(ident, cot[b, rows, :]).astype(BF16)
-            cot_flip_t[b, :, rows] = mm_t(anti, cot[BLOCKS - 1 - b, rows, :]).astype(BF16)
-            columns = slice(b * Q, (b + 1) * Q)
-            part = mm_t(cot[b, rows, :], proj_out[:, columns])
-            part_flip = mm_t(cot[b, rows, :], po_flip[:, columns])
-            forward = part if forward is None else forward + part
-            backward = part_flip if backward is None else backward + part_flip
-        dos[0, rows, :] = forward.astype(BF16)
-        dos[1, rows, :] = backward.astype(BF16)
-        return carry
-
-    lax.fori_loop(0, CHUNKS, cot_step, 0)
+    lax.fori_loop(0, CHUNKS, first_step, 0)
+    for n in range(4, 6):
+        cot_copy(n).wait_recv()
+    lax.fori_loop(0, CHUNKS, last_step, 0)
 
     def grad_step(i, carry):
         strand, k = i // CHUNKS, lax.rem(i, CHUNKS)
@@ -554,6 +580,13 @@
             src, dst = h_send.at[n, :, lax.rem(y + k, 4), :, 0:Q], h_recv.at[n, 0, k - 1]
         return remote(src, dst, S_GPEER + 12 * n + at, peer)
 
+    def x_copy(dz, dy):
+        at = 4 * dz + dy
+        return remote(
+            h_send.at[2, lax.rem(z + dz, 4), lax.rem(y + dy, 4)], last_recv.at[at],
+            S_LAST + at, zy_peer(dz, dy),
+        )
+
     def weight_part(n, left, left_flip, right):
         def step(b, carry):
             value = mm(left[b], right[0]) + mm(left_flip[b], right[1])
@@ -576,8 +609,12 @@
             return carry
 
         lax.fori_loop(0, PEERS, pair_sum, 0)
-        for at in range(6):
-            g_copy(n, at).start()
+        if n == 2:
+            for dz, dy in shifts:
+                x_copy(dz, dy).start()
+        else:
+            for at in range(6):
+                g_copy(n, at).start()
 
     def weight_middle(n):
         for at in range(6):
@@ -706,7 +743,6 @@
     in_sum.near()
     in_sum.middle()
     in_sum.own_block()
-    weight_middle(2)
 
     mix_sum.arrived()
 
@@ -729,7 +765,11 @@
 
     lax.fori_loop(0, CHUNKS, in_step, 0)
 
-    weight_total(2, grad_x)
+    total = g_own[2, z, y]
+    for dz, dy in shifts:
+        x_copy(dz, dy).wait_recv()
+        total = total + last_recv[4 * dz + dy].astype(F32)
+    grad_x[...] = total
 
     for n in range(6):
         cot_copy(n).wait_send()
@@ -739,8 +779,11 @@
     in_sum.drain()
     for n in range(3):
         g_core_copy(n).wait_send()
-        for at in range(12):
-            g_copy(n, at).wait_send()
+    for at in range(12):
+        g_copy(0, at).wait_send()
+        g_copy(1, at).wait_send()
+    for dz, dy in shifts:
+        x_copy(dz, dy).wait_send()
 
 
 def hand_over(*refs):
@@ -774,10 +817,12 @@
     made = pl.pallas_call(
         block_kernel,
         out_shape=results,
-        in_specs=[pl.BlockSpec(memory_space=pl.ANY)] * 5 + [VMEM] * 6,
+        in_specs=[pl.BlockSpec(memory_space=pl.ANY)] * 11,
         out_specs=[VMEM] * 5,
         scratch_shapes=[
             vm((L, D), BF16), vm((D, W), BF16), vm((D, W), BF16), vm((W, D), BF16),
+            vm((NS, D), BF16), vm((NS, D), BF16), vm((HEADS, D), BF16),
+            vm((1, HEADS), F32), vm((1, HEADS), F32), vm((1, HEADS), F32),
             vm((D, W), BF16), vm((D, W), BF16), vm((W, D), BF16), vm((128, D), BF16),
             vm((BLOCKS, Q, L), BF16), vm((BLOCKS, Q, L), BF16),
             vm((BLOCKS, L, Q), BF16), vm((BLOCKS, Q, L), BF16), vm((BLOCKS, Q, L), BF16),
@@ -800,11 +845,11 @@
             vm((2, L, Q), BF16),
             vm((3, 4, 4, ROWS, W), F32), vm((3, 4, 4, ROWS, W), BF16),
             vm((3, 4, 4, ROWS, W), BF16), vm((3, 4, 4, ROWS, W), BF16),
-            vm((3, 2, 3, 4, ROWS, Q), BF16), vm((3, 2, 3, ROWS, Q), BF16),
-            vm((3, 2, 3, ROWS, Q), BF16), vm((3, 2, ROWS, Q), F32),
-            pltpu.SemaphoreType.DMA((5,)),
+            vm((2, 2, 3, 4, ROWS, Q), BF16), vm((2, 2, 3, ROWS, Q), BF16),
+            vm((2, 2, 3, ROWS, Q), BF16), vm((2, 2, ROWS, Q), F32), vm((PEERS, ROWS, W), BF16),
+            pltpu.SemaphoreType.DMA((11,)),
             pltpu.SemaphoreType.DMA((S_ALL,)), pltpu.SemaphoreType.DMA((S_ALL,)),
-            pltpu.SemaphoreType.REGULAR,
+            pltpu.SemaphoreType.REGULAR((3,)),
         ],
         compiler_params=pltpu.CompilerParams(
             vmem_limit_bytes=60 * 2**20, collective_id=0, has_side_effects=True

time: 67.5 us -> 67.1 us (level)
  no operation moved by 1% of the time
where the time goes in v6:
time: 67.1 us; the launch traced here: 66.9 us
  Pallas kernels  66.1 us (99%)
  between operations  0.8 us (1%)
    pallas_call x1, Pallas kernels, body(): pl.pallas_call(block_kernel, out_shape=results, in_specs=[pl.BlockSpec(me...  64 us
    pallas_call x1, Pallas kernels, body(): pl.pallas_call(hand_over, out_shape=results, in_specs=[VMEM] * 5, out_spe...  2.11 us

profile of v6, /device:TPU:1, one launch (start us, length us, event | category | flops | bytes accessed | tf_op | source)
XLA Modules:
  0.0 66.9 jit_solution(9388811669123686903)
XLA Ops:
  0.6 64.0 %block.1 = (bf16[512,256]{1,0:T(8,128)(2,1)}, f32[512,256]{1,0:T(8,128)}, f32[32,512]{1,0:T(8,128)}, f32[32,512]{1,0:T(8,128)}, f32[32,512]{1,0:T(8,128)}) custom-call(bf16[512,1024]{1,0:T(8,128)(2,1)} %hidden_hbm.1, bf16[1024,512]{1,0:T(8,128)(2,1)} %proj_x_hbm.1, bf16[1024,512]{1,0:T(8,128)(2,1)} %proj_z_hbm.1, bf16[512,1024]{1,0:T(8,128)(2,1)} %proj_out_hbm.1, ...), custom_call_target="tpu_custom_call" | custom-call | tf_op jit(solution)/shard_map/block/pallas_call | solution.py:817
  64.7 2.1 %hand_over.1 = (bf16[512,256]{1,0:T(8,128)(2,1)}, f32[512,256]{1,0:T(8,128)}, f32[32,512]{1,0:T(8,128)}, f32[32,512]{1,0:T(8,128)}, f32[32,512]{1,0:T(8,128)}) custom-call(bf16[512,256]{1,0:T(8,128)(2,1)} %get-tuple-element.15.refs_0_, f32[512,256]{1,0:T(8,128)} %get-tuple-element.16.refs_1_, f32[32,512]{1,0:T(8,128)} %get-tuple-element.17.refs_2_, ...), custom_call_target="tpu_custom_call" | custom-call | tf_op jit(solution)/shard_map/hand_over/pallas_call | solution.py:862

commit v7 on v6

--- a/solution.py
+++ b/solution.py
@@ -109,8 +109,8 @@
     block_out, grad_hidden, grad_x, grad_z, grad_out,
     hidden, proj_x, proj_z, proj_out, proj_b, proj_c, proj_dt, bias, rate, skip,
     px_flip, pz_flip, po_flip, small, hidden_t, hidden_flip_t, cot, cot_t, cot_flip_t,
-    xs, zs, bs, cs, dts, dos, cums, dts_soft, e_cums, e_rests, dt_wides, dyb, xdt, zacc,
-    yi, gi, dcs, dbs, dyy, ext, os, dxs, dzs,
+    xs, zs, bs, cs, dts, dos, cums, dts_soft, e_cums, e_rests, dt_wides, dyb, xdt, zacc, kept_decay,
+    yi, dcs, dbs, dyy, ext, os, dzs,
     chunk_state, chunk_grad, chunk_decay, chunk_dot,
     a_msg, a_core, a_pair, a_slots, a_back, a_in,
     b_msg, b_core, b_pair, b_slots, b_back, b_in,
@@ -119,6 +119,7 @@
     g_own, g_send, g_recv, h_send, h_recv, t_send, t_recv, t_own, last_recv,
     load_sem, send_sem, recv_sem, ready_sem,
 ):
+    gi, dxs = zs, dos
     seq, ch = lax.axis_index("seq"), lax.axis_index("ch")
     core, y, z = lax.rem(seq, 2), lax.rem(seq // 2, 4), seq // 8
     other = 1 - core
@@ -169,8 +170,6 @@
         load.start()
     anti = anti_identity()
     e = spread_matrix()
-    loads[0].wait()
-    pl.semaphore_wait(barrier, 7)
     half = [slice(0, Q), slice(Q, L)]
     before, after = lax.rem(ch + 3, 4), lax.rem(ch + 1, 4)
 
@@ -181,8 +180,6 @@
         )[n]
         return remote(cot.at[block, rows], cot.at[block, rows], S_COT + n, x_peer(to))
 
-    for n in range(4):
-        cot_copy(n).start()
     def vouch(n):
         if n:
             pl.semaphore_wait(ready_sem.at[n - 1], 4)
@@ -192,7 +189,6 @@
                     ready_sem.at[n], inc=1, device_id=device, device_id_type=MESH
                 )
 
-    vouch(0)
     for load in loads[5:]:
         load.wait()
     small[...] = jnp.zeros_like(small)
@@ -230,7 +226,11 @@
         return carry
 
     lax.fori_loop(0, CHUNKS, project_step, 0)
-    vouch(1)
+    loads[0].wait()
+    pl.semaphore_wait(barrier, 7)
+    for n in range(4):
+        cot_copy(n).start()
+    vouch(0)
 
     def state_step(i, carry):
         strand, k = i // CHUNKS, lax.rem(i, CHUNKS)
@@ -253,11 +253,7 @@
         return carry
 
     lax.fori_loop(0, 2 * CHUNKS, state_step, 0)
-    vouch(2)
-
-    for n in range(2):
-        cot_copy(n).wait_recv()
-        cot_copy(4 + n).start()
+    vouch(1)
 
     def times(strand):
         return list(range(CHUNKS)) if strand == 0 else list(range(CHUNKS))[::-1]
@@ -374,10 +370,10 @@
     def within_step(i, carry):
         strand, k = i // CHUNKS, lax.rem(i, CHUNKS)
         rows = rows_of(k)
-        mask = order(1 - 2 * strand)
+        mask = order(2 * strand - 1)
         cum = cums[strand, rows, :]
         cum_t = cum.T
-        scores = mm_t(cs[strand, rows, :], bs[strand, rows, :])
+        scores = mm_t(bs[strand, rows, :], cs[strand, rows, :])
         for pair in range(HEADS // 2):
             columns = slice(pair * 128, (pair + 1) * 128)
             x_pair = xdt[strand, rows, columns]
@@ -387,13 +383,22 @@
                 own = (lane >= HEAD) if odd else (lane < HEAD)
                 x_own = jnp.where(own, x_pair, jnp.zeros((), BF16))
                 decay = jnp.exp(
-                    jnp.where(mask, cum[:, h : h + 1] - cum_t[h : h + 1, :], -1e30)
+                    jnp.where(mask, cum_t[h : h + 1, :] - cum[:, h : h + 1], -1e30)
                 )
-                y_new = mm((decay * scores).astype(BF16), x_own)
+                mixing = (decay * scores).astype(BF16)
+                kept_decay[i, h] = decay.astype(BF16)
+                y_new = t_mm(mixing, x_own)
                 y_sum = y_new if y_sum is None else y_sum + y_new
             yi[strand, rows, columns] = y_sum
 
         @pl.when(i == 0)
+        def _():
+            vouch(2)
+            for n in range(2):
+                cot_copy(n).wait_recv()
+                cot_copy(4 + n).start()
+
+        @pl.when(i == 1)
         def _():
             vouch(3)
             round_a.spread_out()
@@ -418,14 +423,16 @@
         rows = rows_of(k)
         parts = [cot_block(c, rows) for c in (ch, before, after)]
         for strand in range(2):
-            gi[strand, rows, :] = sum(part[strand] for part in parts)
+            value = sum(part[strand] for part in parts)
+            g_own[strand, pl.ds(2 * k, 2)] = value.reshape(2, 4, ROWS, W)
         return carry
 
     def last_step(k, carry):
         rows = rows_of(k)
         parts = cot_block(lax.rem(ch + 2, 4), rows)
         for strand in range(2):
-            dos[strand, rows, :] = (gi[strand, rows, :] + parts[strand]).astype(BF16)
+            early = g_own[strand, pl.ds(2 * k, 2)].reshape(Q, W)
+            dos[strand, rows, :] = (early + parts[strand]).astype(BF16)
         return carry
 
     for n in range(2, 4):
@@ -652,9 +659,6 @@
     def inner_step(i, carry):
         strand, k = i // CHUNKS, lax.rem(i, CHUNKS)
         rows = rows_of(k)
-        mask = order(2 * strand - 1)
-        cum = cums[strand, rows, :]
-        cum_t = cum.T
         b = bs[strand, rows, :]
         c = cs[strand, rows, :]
         scores = mm_t(b, c)
@@ -666,14 +670,12 @@
                 h = 2 * pair + odd
                 own = (lane >= HEAD) if odd else (lane < HEAD)
                 dy_own = jnp.where(own, dy_pair, jnp.zeros((), BF16))
-                decay = jnp.exp(
-                    jnp.where(mask, cum_t[h : h + 1, :] - cum[:, h : h + 1], -1e30)
-                )
-                cross = mm_t(x_pair, dy_own)
+                decay = kept_decay[i, h].astype(F32)
+                part = decay * mm_t(x_pair, dy_own)
                 if h == 0:
-                    zacc[...] = decay * cross
+                    zacc[...] = part
                 else:
-                    zacc[...] += decay * cross
+                    zacc[...] += part
                 g_new = mm((decay * scores).astype(BF16), dy_own)
                 g_sum = g_new if g_sum is None else g_sum + g_new
             gi[strand, rows, columns] = g_sum
@@ -830,9 +832,10 @@
             vm((2, L, HEADS), F32), vm((2, L, W), BF16), vm((2, L, HEADS), F32),
             vm((2, L, HEADS), F32), vm((2, L, W), F32), vm((2, L, W), F32), vm((2, L, W), F32),
             vm((2, L, W), BF16), vm((2, L, W), BF16), vm((Q, Q), F32),
-            vm((2, L, W), F32), vm((2, L, W), F32), vm((2, L, NS), F32), vm((2, L, NS), F32),
+            vm((2 * CHUNKS, HEADS, Q, Q), BF16),
+            vm((2, L, W), F32), vm((2, L, NS), F32), vm((2, L, NS), F32),
             vm((2, L, HEADS), F32),
-            vm((L, 128), BF16), vm((2, L, W), BF16), vm((2, L, W), BF16), vm((2, L, W), BF16),
+            vm((L, 128), BF16), vm((2, L, W), BF16), vm((2, L, W), BF16),
             vm((2, CHUNKS, NS, W), F32), vm((2, CHUNKS, NS, W), F32),
             vm((2, CHUNKS, 8, W), F32), vm((2, CHUNKS, NS, W), F32),
             vm((2, 40, Q), F32), vm((40, Q), F32), vm((2, 24, Q), F32), vm((PEERS, 24, Q), F32),

time: 67.1 us -> 67.4 us (level)
  no operation moved by 1% of the time
where the time goes in v7:
time: 67.4 us; the launch traced here: 67.3 us
  Pallas kernels  66.5 us (99%)
  between operations  0.8 us (1%)
    pallas_call x1, Pallas kernels, body(): pl.pallas_call(block_kernel, out_shape=results, in_specs=[pl.BlockSpec(me...  64.3 us
    pallas_call x1, Pallas kernels, body(): pl.pallas_call(hand_over, out_shape=results, in_specs=[VMEM] * 5, out_spe...  2.11 us

profile of v7, /device:TPU:1, one launch (start us, length us, event | category | flops | bytes accessed | tf_op | source)
XLA Modules:
  0.0 67.3 jit_solution(11086047375214876669)
XLA Ops:
  0.6 64.3 %block.1 = (bf16[512,256]{1,0:T(8,128)(2,1)}, f32[512,256]{1,0:T(8,128)}, f32[32,512]{1,0:T(8,128)}, f32[32,512]{1,0:T(8,128)}, f32[32,512]{1,0:T(8,128)}) custom-call(bf16[512,1024]{1,0:T(8,128)(2,1)} %hidden_hbm.1, bf16[1024,512]{1,0:T(8,128)(2,1)} %proj_x_hbm.1, bf16[1024,512]{1,0:T(8,128)(2,1)} %proj_z_hbm.1, bf16[512,1024]{1,0:T(8,128)(2,1)} %proj_out_hbm.1, ...), custom_call_target="tpu_custom_call" | custom-call | tf_op jit(solution)/shard_map/block/pallas_call | solution.py:819
  65.0 2.1 %hand_over.1 = (bf16[512,256]{1,0:T(8,128)(2,1)}, f32[512,256]{1,0:T(8,128)}, f32[32,512]{1,0:T(8,128)}, f32[32,512]{1,0:T(8,128)}, f32[32,512]{1,0:T(8,128)}) custom-call(bf16[512,256]{1,0:T(8,128)(2,1)} %get-tuple-element.15.refs_0_, f32[512,256]{1,0:T(8,128)} %get-tuple-element.16.refs_1_, f32[32,512]{1,0:T(8,128)} %get-tuple-element.17.refs_2_, ...), custom_call_target="tpu_custom_call" | custom-call | tf_op jit(solution)/shard_map/hand_over/pallas_call | solution.py:865

commit v8 on v7

--- a/solution.py
+++ b/solution.py
@@ -683,25 +683,20 @@
         dbs[strand, rows, :] = mm(pairs, c)
         dcs[strand, rows, :] += t_mm(pairs, b)
 
-        @pl.when(i == 0)
+        @pl.when(i == 1)
         def _():
             mix_sum.middle()
             weight_pair(1)
 
-        @pl.when(i == 1)
+        @pl.when(i == 2)
         def _():
             round_b.collect()
 
-        @pl.when(i == 2)
-        def _():
-            weight_middle(0)
-
         return carry
 
     lax.fori_loop(0, 2 * CHUNKS, inner_step, 0)
 
     mix_sum.own_block()
-    weight_middle(1)
 
     up, down = round_b.take()
     for strand, grad in enumerate((down, up)):
@@ -741,10 +736,12 @@
 
     weight_part(2, hidden_t, hidden_flip_t, dxs)
     in_sum.far()
+    in_sum.near()
     weight_pair(2)
-    in_sum.near()
     in_sum.middle()
     in_sum.own_block()
+    weight_middle(0)
+    weight_middle(1)
 
     mix_sum.arrived()
 

time: 67.4 us -> 67.4 us (level)
  no operation moved by 1% of the time
where the time goes in v8:
time: 67.4 us; the launch traced here: 67.3 us
  Pallas kernels  66.6 us (99%)
    pallas_call x1, Pallas kernels, body(): pl.pallas_call(block_kernel, out_shape=results, in_specs=[pl.BlockSpec(me...  64.5 us
    pallas_call x1, Pallas kernels, body(): pl.pallas_call(hand_over, out_shape=results, in_specs=[VMEM] * 5, out_spe...  2.11 us

profile of v8, /device:TPU:1, one launch (start us, length us, event | category | flops | bytes accessed | tf_op | source)
XLA Modules:
  0.0 67.3 jit_solution(9407388161122739706)
XLA Ops:
  0.6 64.5 %block.1 = (bf16[512,256]{1,0:T(8,128)(2,1)}, f32[512,256]{1,0:T(8,128)}, f32[32,512]{1,0:T(8,128)}, f32[32,512]{1,0:T(8,128)}, f32[32,512]{1,0:T(8,128)}) custom-call(bf16[512,1024]{1,0:T(8,128)(2,1)} %hidden_hbm.1, bf16[1024,512]{1,0:T(8,128)(2,1)} %proj_x_hbm.1, bf16[1024,512]{1,0:T(8,128)(2,1)} %proj_z_hbm.1, bf16[512,1024]{1,0:T(8,128)(2,1)} %proj_out_hbm.1, ...), custom_call_target="tpu_custom_call" | custom-call | tf_op jit(solution)/shard_map/block/pallas_call | solution.py:816
  65.2 2.1 %hand_over.1 = (bf16[512,256]{1,0:T(8,128)(2,1)}, f32[512,256]{1,0:T(8,128)}, f32[32,512]{1,0:T(8,128)}, f32[32,512]{1,0:T(8,128)}, f32[32,512]{1,0:T(8,128)}) custom-call(bf16[512,256]{1,0:T(8,128)(2,1)} %get-tuple-element.15.refs_0_, f32[512,256]{1,0:T(8,128)} %get-tuple-element.16.refs_1_, f32[32,512]{1,0:T(8,128)} %get-tuple-element.17.refs_2_, ...), custom_call_target="tpu_custom_call" | custom-call | tf_op jit(solution)/shard_map/hand_over/pallas_call | solution.py:862
